TPU v7x, 32 devices: a whole 2x2x4 slice. The times are simulated.
32 devices in a mesh: slab: 8 (over z, y), head: 4 (over x, core).
Axes of the slice: x: 2, y: 2, z: 4, core: 2. Of those that a mesh axis runs over, the one named last changes fastest.
Arguments:
- tokens: bfloat16 [16384, 384], P(('slab', 'head')), may hold values from -6 to 6
- norm_gain: float32 [384], replicated, may hold values from 0.25 to 1.75
- w_qkv: bfloat16 [3, 384, 384], replicated, may hold values from -0.3125 to 0.3125
- w_out: bfloat16 [384, 384], replicated, may hold values from -0.625 to 0.625
- cotangent: bfloat16 [16384, 384], P(('slab', 'head')), may hold values from -6 to 6
- neighbours: int32 [128, 8], P('slab'), may hold values from 0 to 127, as said below
- counts: int32 [128], P('slab'), may hold values from 2 to 8, as said below
Outputs:
- output: bfloat16 [16384, 384], P(('slab', 'head'))
- d_tokens: bfloat16 [16384, 384], P(('slab', 'head'))
- d_w_qkv: float32 [3, 384, 384], P(None, None, 'head')
- d_w_out: float32 [384, 384], replicated
- d_gain: float32 [384], replicated
Inputs may be any that keep to these rules, and one draw needn't show every extreme that they name: `neighbours`: entry 0 of block b's list is b itself; the entries of a list are distinct and each lies within 16 blocks of b along the periodic block order (modulo 128); every block lists one block at distance exactly 16. Only the first counts[b] slots of block b's list are live; the first block of every slab has all 8 live.
All inputs are finite; a program needn't handle non-finite values.
Results may differ from a plain program's by a relative error of at most 0.024.
Values may be sent and summed in bfloat16 or wider, within the bound.
A program may use at most 192 MiB of HBM per device.

v0:
```python
import math

import jax
import jax.numpy as jnp
from jax import lax
from jax.sharding import PartitionSpec as P

HEADS = 12
BLK = 128
REACH = 16


exponent_divisor = 10.0
norm_eps = 1e-06


def padded(value, sides, width):
    for axis, dim in sides:
        size, length = (lax.axis_size(axis), value.shape[dim])
        up = [(i, (i + 1) % size) for i in range(size)]
        down = [(j, i) for i, j in up]
        last = lax.slice_in_dim(value, length - width, length, axis=dim)
        first = lax.slice_in_dim(value, 0, width, axis=dim)
        before = lax.ppermute(last, axis, up)
        after = lax.ppermute(first, axis, down)
        value = jnp.concatenate([before, value, after], axis=dim)
    return value


def passed_along(value, axis, steps):
    count = lax.axis_size(axis)
    pairs = [(source, (source + steps) % count) for source in range(count)]
    return lax.ppermute(value, axis, pairs)


def normalize(projected, head_dim):
    by_head = projected.reshape(projected.shape[:-1] + (projected.shape[-1] // head_dim, head_dim))
    length = jnp.sqrt(jnp.sum(by_head * by_head, -1, keepdims=True))
    divisor = jnp.maximum(length, 0.7 * math.sqrt(head_dim))
    return (by_head / divisor, divisor, length > 0.7 * math.sqrt(head_dim))


def unit_heads(projected, head_dim):
    unit, divisor, active = normalize(projected, head_dim)
    return unit.reshape(projected.shape)


def norm_back(projected, grad, head_dim):
    unit, divisor, active = normalize(projected, head_dim)
    along = grad.astype(jnp.float32).reshape(unit.shape)
    inner = jnp.sum(unit * along, -1, keepdims=True)
    result = (along - jnp.where(active, unit * inner, 0.0)) / divisor
    return result.reshape(projected.shape)


def attention_weights(asking_matrix, lookup_matrix, counts):
    slot_ids = jnp.arange(lookup_matrix.shape[1], dtype=jnp.int32) // asking_matrix.shape[1]
    raw_affinity = exponent_divisor * jnp.einsum(
        "pcxt,pqxt->pxcq", asking_matrix, lookup_matrix, preferred_element_type=jnp.float32
    )
    live_mask = (slot_ids[None, :] < counts[:, None]).astype(jnp.float32)
    raised = jnp.exp(raw_affinity) * live_mask[:, None, None, :]
    return raised / jnp.sum(raised, -1, keepdims=True)


def local(tokens, norm_gain, w_qkv, w_out, cotangent, neighbours, counts):
    width = tokens.shape[1]
    head_dim = width // HEADS
    n_head = lax.axis_size("head")
    n_slab = lax.axis_size("slab")
    head_cols = width // n_head
    heads_here = HEADS // n_head
    head_index = lax.axis_index("head")
    slab_index = lax.axis_index("slab")
    slab_blocks, n_slots = neighbours.shape
    block_rows = BLK
    slab_rows = slab_blocks * block_rows
    tok_f32 = tokens.astype(jnp.float32)
    inverse = lax.rsqrt(jnp.mean(tok_f32 * tok_f32, -1, keepdims=True) + norm_eps)
    normed = (tok_f32 * inverse * norm_gain).astype(jnp.bfloat16)
    w_here = lax.dynamic_slice_in_dim(w_qkv, head_index * head_cols, head_cols, 2)
    gathered = lax.all_gather(normed, "head", axis=0, tiled=True)
    projected = jnp.einsum("rd,cde->cre", gathered, w_here, preferred_element_type=jnp.float32)
    packed = jnp.stack(
        [unit_heads(projected[0], head_dim), unit_heads(projected[1], head_dim), projected[2]]
    ).astype(jnp.bfloat16)
    q_heads = packed[0]
    keys_values = packed[1:]
    extended = padded(keys_values, (("slab", 1),), REACH * block_rows)
    ext_blocks = slab_blocks + 2 * REACH
    n_blocks = slab_blocks * n_slab
    lookup = (neighbours - slab_index * slab_blocks + REACH) % n_blocks
    group_size = 8
    n_groups = slab_blocks // group_size
    key_blocks = extended.reshape(2, ext_blocks, block_rows, heads_here, head_dim)
    query_groups = q_heads.reshape(n_groups, group_size, block_rows, heads_here, head_dim)
    lookup_groups = lookup.reshape(n_groups, group_size, n_slots)
    count_groups = counts.reshape(n_groups, group_size)

    def fetch(lookup_rows):
        both = key_blocks[:, lookup_rows.reshape(-1)]
        return both.reshape(2, group_size, n_slots * block_rows, heads_here, head_dim)

    def attend(inputs):
        asking_matrix, lookup_rows, live = inputs
        both = fetch(lookup_rows)
        weights_bf = attention_weights(asking_matrix, both[0], live).astype(jnp.bfloat16)
        result = jnp.einsum(
            "ghqk,gkhd->gqhd", weights_bf, both[1], preferred_element_type=jnp.float32
        )
        return result.astype(jnp.bfloat16)

    attended_heads = lax.map(attend, (query_groups, lookup_groups, count_groups)).reshape(
        slab_rows, head_cols
    )
    attended = lax.all_to_all(attended_heads, "head", split_axis=0, concat_axis=1, tiled=True)
    output = (tok_f32 + jnp.dot(attended, w_out, preferred_element_type=jnp.float32)).astype(
        jnp.bfloat16
    )
    d_out_part = jnp.dot(attended.T, cotangent, preferred_element_type=jnp.float32)
    d_attended = jnp.dot(cotangent, w_out.T, preferred_element_type=jnp.float32).astype(
        jnp.bfloat16
    )
    d_heads = lax.all_to_all(d_attended, "head", split_axis=1, concat_axis=0, tiled=True)
    d_groups = d_heads.reshape(n_groups, group_size, block_rows, heads_here, head_dim)

    def backward_group(grad_buffer, inputs):
        asking_matrix, d_attn, lookup_rows, live = inputs
        both = fetch(lookup_rows)
        normalized_affinity = attention_weights(asking_matrix, both[0], live)
        weights_bf = normalized_affinity.astype(jnp.bfloat16)
        affinity_share_cotangent = jnp.einsum(
            "pcxt,pqxt->pxcq", d_attn, both[1], preferred_element_type=jnp.float32
        )
        pairwise_dot_sum = jnp.sum(
            affinity_share_cotangent * normalized_affinity, -1, keepdims=True
        )
        affinity_cotangent = (
            exponent_divisor * normalized_affinity * (affinity_share_cotangent - pairwise_dot_sum)
        ).astype(jnp.bfloat16)
        d_query = jnp.einsum(
            "ghqk,gkhd->gqhd", affinity_cotangent, both[0], preferred_element_type=jnp.float32
        )
        d_keys = jnp.einsum(
            "ghqk,gqhd->gkhd", affinity_cotangent, asking_matrix, preferred_element_type=jnp.float32
        )
        d_values = jnp.einsum(
            "ghqk,gqhd->gkhd", weights_bf, d_attn, preferred_element_type=jnp.float32
        )
        stacked = jnp.stack([d_keys, d_values]).reshape(
            2, group_size * n_slots, block_rows, heads_here, head_dim
        )
        grad_buffer = grad_buffer.at[:, lookup_rows.reshape(-1)].add(stacked)
        return (grad_buffer, d_query)

    start_buffer = jnp.zeros((2, ext_blocks, block_rows, heads_here, head_dim), jnp.float32)
    grad_buffer, d_query_groups = lax.scan(
        backward_group, start_buffer, (query_groups, d_groups, lookup_groups, count_groups)
    )
    low_rim = grad_buffer[:, :REACH]
    high_rim = grad_buffer[:, REACH + slab_blocks :]
    from_above = passed_along(low_rim.astype(jnp.bfloat16), "slab", -1).astype(low_rim.dtype)
    from_below = passed_along(high_rim, "slab", 1)
    own_grads = grad_buffer[:, REACH : REACH + slab_blocks]
    own_grads = own_grads.at[:, slab_blocks - REACH :].add(from_above)
    own_grads = own_grads.at[:, :REACH].add(from_below)
    d_packed = jnp.concatenate(
        [
            d_query_groups.reshape(1, slab_rows, head_cols),
            own_grads.reshape(2, slab_rows, head_cols),
        ],
        0,
    ).astype(jnp.bfloat16)
    d_query_part = norm_back(projected[0], d_packed[0], head_dim).astype(jnp.bfloat16)
    d_key_part = norm_back(projected[1], d_packed[1], head_dim).astype(jnp.bfloat16)
    d_qkv = jnp.stack([d_query_part, d_key_part, d_packed[2]])
    d_normed = lax.psum_scatter(
        jnp.einsum("crk,cdk->rd", d_qkv, w_here, preferred_element_type=jnp.float32).astype(
            jnp.bfloat16
        ),
        "head",
        scatter_dimension=0,
        tiled=True,
    ).astype(jnp.float32)
    d_qkv_part = jnp.einsum("rd,crk->cdk", gathered, d_qkv, preferred_element_type=jnp.float32)
    d_w_qkv = lax.psum(d_qkv_part.astype(jnp.bfloat16), "slab").astype(jnp.float32)
    d_gain_part = jnp.sum(d_normed * tok_f32 * inverse, 0)
    d_w_out, d_gain = lax.psum((d_out_part, d_gain_part), ("slab", "head"))
    scaled = d_normed * norm_gain
    d_tokens = (
        cotangent.astype(jnp.float32)
        + inverse * scaled
        - tok_f32 * inverse**3 * jnp.mean(scaled * tok_f32, -1, keepdims=True)
    )
    return (output, d_tokens.astype(jnp.bfloat16), d_w_qkv, d_w_out, d_gain)


def solution(mesh):
    placed = (
        P(("slab", "head"), None),
        P(),
        P(),
        P(),
        P(("slab", "head"), None),
        P("slab", None),
        P("slab"),
    )
    return jax.shard_map(
        local,
        mesh=mesh,
        in_specs=placed,
        out_specs=(
            P(("slab", "head"), None),
            P(("slab", "head"), None),
            P(None, None, "head"),
            P(),
            P(),
        ),
        check_vma=False,
    )
```

profile of v0, /device:TPU:0, one launch (start us, length us, event | category | flops | bytes accessed | tf_op | source)
XLA Modules:
  0.0 697.3 jit_solution(6902024988808929098)
XLA Ops:
  11.5 22.5 %all-gather.2.cloned.1.call-done = bf16[2048,384]{1,0:T(8,128)(2,1)} async-done(((bf16[512,384]{1,0:T(8,128)(2,1)}), bf16[2048,384]{1,0:T(8,128)(2,1)}) %all-gather.2.cloned.1.call-update) | async-done | bytes 1572880 | tf_op jit(solution)/shard_map/all_gather | solution.py:82
  34.0 2.5 convolution_bitcast_fusion.2
  40.6 3.2 collective-permute-start.1
  45.0 3.5 all-to-all-start.1
  48.7 7.2 %all-to-all-done.1 = bf16[512,4,96]{0,2,1:T(8,128)(2,1)S(1)} async-done(((bf16[512,4,96]{0,2,1:T(8,128)(2,1)}), bf16[512,4,96]{0,2,1:T(8,128)(2,1)S(1)}, u32[]{:S(2)}, u32[]{:S(2)}) %all-to-all-start.1) | async-done | bytes 393248 | tf_op jit(solution)/shard_map/all_to_all | solution.py:124
  56.5 18.4 %collective-permute-done = bf16[2,2048,96]{1,2,0:T(8,128)(2,1)} collective-permute-done((bf16[2,2048,96]{1,2,0:T(8,128)(2,1)}, bf16[2,2048,96]{1,2,0:T(8,128)(2,1)}, u32[]{:S(2)}, u32[]{:S(2)}) %collective-permute-start) | collective-permute-done | bytes 786464 | tf_op jit(solution)/shard_map/ppermute | solution.py:24
  74.9 2.2 collective-permute-done.1
  78.7 2.0 copy.92
  80.7 13.4 %copy.64 = bf16[2,48,128,3,32]{4,3,2,1,0:T(4,128)(2,1)} copy(bf16[2,48,128,3,32]{2,1,4,3,0:T(8,128)(2,1)} %bitcast.220) | data formatting | bytes 4718592 | tf_op jit(solution)/shard_map/while | solution.py:113
  94.1 2.7 broadcast_in_dim.68
  96.8 270.6 %while.31 = (s32[]{:T(128)}, f32[2,48,128,3,32]{2,4,3,1,0:T(8,128)}, bf16[2,8,128,3,32]{2,4,3,1,0:T(8,128)(2,1)}, s32[2,8,8]{2,1,0:T(8,128)S(1)}, bf16[2,8,128,3...) while((s32[]{:T(128)}, ...), condition=%wide.region_10.11_spmd, body=%wide.region_6.10_spmd.sunk | while | flops 1069567168 | bytes 201579056 | solution.py:157
  111.0 20.9 %gather_fusion.1 = bf16[64,2,128,3,32]{4,3,2,1,0:T(4,128)(2,1)} fusion(bf16[2,48,128,3,32]{4,3,2,1,0:T(4,128)(2,1)} %get-tuple-element.475, s32[1024]{0:T(1024)S(1)} %pad_clamp_fusion.5), kind=kCustom, calls=%fused_computation.1.clone.1 | custom fusion | bytes 6291712 | tf_op jit(solution)/shard_map/while/body/eval_jaxpr/gather | solution.py:101
  131.9 16.0 %fusion.128 = (bf16[1,64,128,3,32]{4,3,2,0,1:T(4,128)(2,1)}, bf16[1,64,128,3,32]{4,3,2,0,1:T(4,128)(2,1)}) fusion(bf16[2,64,128,3,32]{4,3,2,0,1:T(4,128)(2,1)} %bitcast.214), kind=kLoop, calls=%fused_computation.145.clone.1 | loop fusion | bytes 6291456 | tf_op jit(solution)/shard_map/while/body/eval_jaxpr/slice | solution.py:133
  147.9 10.5 %copy.130 = bf16[8,1024,3,32]{1,3,2,0:T(8,128)(2,1)S(1)} copy(bf16[8,1024,3,32]{3,2,1,0:T(4,128)(2,1)} %bitcast.216) | data formatting | bytes 3145728 | tf_op jit(solution)/shard_map/while/body/eval_jaxpr/squeeze | solution.py:130
  158.5 6.6 fusion.129
  165.1 12.4 %multiply_reduce_fusion.6 = (f32[8,3,128]{2,1,0:T(4,128)S(1)}, f32[8,3,128,1024]{3,2,1,0:T(8,128)}) fusion(f32[8,3,128]{2,1,0:T(4,128)S(1)} %get-tuple-element.427, f32[8,1024]{1,0:T(8,128)S(1)} %compare_convert_fusion.5, f32[8,3,128,1024]{3,2,1,0:T(8,128)} %get-tuple-element.426, bf16[8,1024,3,32]{3,2,1,0:T(4,128)(2,1)S(1)} %bitcast.218, ...), kind=kOutput, calls=%fused_computation.32.clone.1 | convolution fusion | flops 217052160 | bytes 26992640 | tf_op jit(solution)/shard_map/while/body/eval_jaxpr/pcxt,pqxt->pxcq/dot_general | solution.py:132
  177.5 9.8 %multiply_convert_fusion.2 = bf16[8,3,128,1024]{3,2,1,0:T(8,128)(2,1)S(1)} fusion(f32[8,3,128,1024]{3,2,1,0:T(8,128)} %get-tuple-element.429, f32[8,3,128]{2,1,0:T(4,128)S(1)} %get-tuple-element.430, f32[8,3,128]{2,1,0:T(4,128)S(1)} %get-tuple-element.427, f32[8,1024]{1,0:T(8,128)S(1)} %compare_convert_fusion.5, ...), kind=kLoop, calls=%fused_computation.31.clone.1 | loop fusion | flops 22020096 | bytes 31514624 | tf_op jit(solution)/shard_map/while/body/eval_jaxpr/convert_element_type | solution.py:140
  187.3 2.3 fusion.131
  190.6 3.5 copy.132
  194.1 4.6 stack.23
  198.6 5.9 fusion.130
  204.6 3.5 copy.131
  208.1 4.5 stack.22
  212.7 3.4 maximum_bitcast_fusion.2
  216.1 6.3 copy.133
  222.4 16.6 %scatter_fusion = f32[2,48,128,3,32]{2,4,3,1,0:T(8,128)} fusion(f32[2,48,128,3,32]{2,4,3,1,0:T(8,128)} %get-tuple-element.462, s32[64]{0:T(128)S(1)} %fusion.126, f32[64,2,128,3,32]{2,4,3,1,0:T(8,128)} %copy.133), kind=kCustom, calls=%fused_computation.2.clone.1 | custom fusion | flops 1572864 | bytes 18874624 | tf_op jit(solution)/shard_map/while/body/eval_jaxpr/scatter-add | solution.py:153
  239.1 20.9 %gather_fusion.1 = bf16[64,2,128,3,32]{4,3,2,1,0:T(4,128)(2,1)} fusion(bf16[2,48,128,3,32]{4,3,2,1,0:T(4,128)(2,1)} %get-tuple-element.475, s32[1024]{0:T(1024)S(1)} %pad_clamp_fusion.5), kind=kCustom, calls=%fused_computation.1.clone.1 | custom fusion | bytes 6291712 | tf_op jit(solution)/shard_map/while/body/eval_jaxpr/gather | solution.py:101
  260.0 16.0 %fusion.128 = (bf16[1,64,128,3,32]{4,3,2,0,1:T(4,128)(2,1)}, bf16[1,64,128,3,32]{4,3,2,0,1:T(4,128)(2,1)}) fusion(bf16[2,64,128,3,32]{4,3,2,0,1:T(4,128)(2,1)} %bitcast.214), kind=kLoop, calls=%fused_computation.145.clone.1 | loop fusion | bytes 6291456 | tf_op jit(solution)/shard_map/while/body/eval_jaxpr/slice | solution.py:133
  276.0 10.5 %copy.130 = bf16[8,1024,3,32]{1,3,2,0:T(8,128)(2,1)S(1)} copy(bf16[8,1024,3,32]{3,2,1,0:T(4,128)(2,1)} %bitcast.216) | data formatting | bytes 3145728 | tf_op jit(solution)/shard_map/while/body/eval_jaxpr/squeeze | solution.py:130
  286.6 6.6 fusion.129
  293.2 12.4 %multiply_reduce_fusion.6 = (f32[8,3,128]{2,1,0:T(4,128)S(1)}, f32[8,3,128,1024]{3,2,1,0:T(8,128)}) fusion(f32[8,3,128]{2,1,0:T(4,128)S(1)} %get-tuple-element.427, f32[8,1024]{1,0:T(8,128)S(1)} %compare_convert_fusion.5, f32[8,3,128,1024]{3,2,1,0:T(8,128)} %get-tuple-element.426, bf16[8,1024,3,32]{3,2,1,0:T(4,128)(2,1)S(1)} %bitcast.218, ...), kind=kOutput, calls=%fused_computation.32.clone.1 | convolution fusion | flops 217052160 | bytes 26992640 | tf_op jit(solution)/shard_map/while/body/eval_jaxpr/pcxt,pqxt->pxcq/dot_general | solution.py:132
  305.6 9.8 %multiply_convert_fusion.2 = bf16[8,3,128,1024]{3,2,1,0:T(8,128)(2,1)S(1)} fusion(f32[8,3,128,1024]{3,2,1,0:T(8,128)} %get-tuple-element.429, f32[8,3,128]{2,1,0:T(4,128)S(1)} %get-tuple-element.430, f32[8,3,128]{2,1,0:T(4,128)S(1)} %get-tuple-element.427, f32[8,1024]{1,0:T(8,128)S(1)} %compare_convert_fusion.5, ...), kind=kLoop, calls=%fused_computation.31.clone.1 | loop fusion | flops 22020096 | bytes 31514624 | tf_op jit(solution)/shard_map/while/body/eval_jaxpr/convert_element_type | solution.py:140
  315.4 2.3 fusion.131
  318.7 3.5 copy.132
  322.2 4.6 stack.23
  326.7 5.9 fusion.130
  332.7 3.5 copy.131
  336.2 4.5 stack.22
  340.8 3.4 maximum_bitcast_fusion.2
  344.2 6.3 copy.133
  350.5 16.6 %scatter_fusion = f32[2,48,128,3,32]{2,4,3,1,0:T(8,128)} fusion(f32[2,48,128,3,32]{2,4,3,1,0:T(8,128)} %get-tuple-element.462, s32[64]{0:T(128)S(1)} %fusion.126, f32[64,2,128,3,32]{2,4,3,1,0:T(8,128)} %copy.133), kind=kCustom, calls=%fused_computation.2.clone.1 | custom fusion | flops 1572864 | bytes 18874624 | tf_op jit(solution)/shard_map/while/body/eval_jaxpr/scatter-add | solution.py:153
  367.5 2.8 slice.135
  370.3 2.5 slice.163
  372.8 4.6 collective-permute-start.2
  381.4 2.2 fusion.44
  383.6 41.9 %collective-permute-done.2 = bf16[2,16,128,3,32]{2,4,3,1,0:T(8,128)(2,1)} collective-permute-done((bf16[2,16,128,3,32]{2,4,3,1,0:T(8,128)(2,1)}, bf16[2,16,128,3,32]{2,4,3,1,0:T(8,128)(2,1)}, u32[]{:S(2)}, u32[]{:S(2)}) %collective-permute-start.2) | collective-permute-done | bytes 786464 | tf_op jit(solution)/shard_map/ppermute | solution.py:33
  425.5 2.5 add_convert_fusion
  431.4 2.2 fusion.43
  435.7 2.9 fusion.60
  439.5 2.5 fusion.52
  442.0 3.5 bitcast_convert_fusion
  445.7 102.6 %while.30 = (s32[]{:T(128)}, bf16[2,8,128,3,32]{2,1,0,4,3:T(8,128)(2,1)S(1)}, s32[2,8,8]{2,1,0:T(8,128)S(1)}, bf16[2,48,128,3,32]{4,3,2,1,0:T(4,128)(2,1)}, bf16...) while((s32[]{:T(128)}, bf16[2,8,128,3,32]{2,1,0,4,3:T(8,128)(2,1)S(1)}, ...), condition=%wide.region_5.6_spmd, body=%wide.region_3.5_spmd.sunk | while | flops 424794304 | bytes 48634044 | solution.py:113
  446.0 20.9 %gather_fusion = bf16[64,2,128,3,32]{4,3,2,1,0:T(4,128)(2,1)} fusion(bf16[2,48,128,3,32]{4,3,2,1,0:T(4,128)(2,1)} %get-tuple-element.448, s32[1024]{0:T(1024)S(1)} %pad_clamp_fusion.4), kind=kCustom, calls=%fused_computation.clone.1 | custom fusion | bytes 6291712 | tf_op jit(solution)/shard_map/while/body/eval_jaxpr/gather | solution.py:101
  466.9 13.2 %fusion.117 = (bf16[1,64,128,3,32]{4,3,2,0,1:T(4,128)(2,1)}, bf16[1,64,128,3,32]{4,3,2,0,1:T(4,128)(2,1)S(1)}) fusion(bf16[2,64,128,3,32]{4,3,2,0,1:T(4,128)(2,1)} %bitcast.215), kind=kLoop, calls=%fused_computation.144.clone.1 | loop fusion | bytes 6291456 | tf_op jit(solution)/shard_map/while/body/eval_jaxpr/slice | solution.py:109
  480.2 6.3 fusion.118
  486.5 10.3 %fusion.119 = bf16[1,8,128,3,32]{2,4,3,1,0:T(8,128)(2,1)S(1)} fusion(f32[8,3,128,1024]{3,2,1,0:T(8,128)} %get-tuple-element.414, f32[8,3,128]{2,1,0:T(4,128)S(1)} %get-tuple-element.415, f32[8,1024]{1,0:T(8,128)S(1)} %compare_convert_fusion.4, bf16[8,1024,3,32]{3,2,1,0:T(4,128)(2,1)} %bitcast.219), kind=kOutput, calls=%fused_computation.11.clone.1 | convolution fusion | flops 214007808 | bytes 14397440 | tf_op jit(solution)/shard_map/while/body/eval_jaxpr/ghqk,gkhd->gqhd/dot_general | solution.py:108
  497.1 21.0 %gather_fusion = bf16[64,2,128,3,32]{4,3,2,1,0:T(4,128)(2,1)} fusion(bf16[2,48,128,3,32]{4,3,2,1,0:T(4,128)(2,1)} %get-tuple-element.448, s32[1024]{0:T(1024)S(1)} %pad_clamp_fusion.4), kind=kCustom, calls=%fused_computation.clone.1 | custom fusion | bytes 6291712 | tf_op jit(solution)/shard_map/while/body/eval_jaxpr/gather | solution.py:101
  518.1 13.2 %fusion.117 = (bf16[1,64,128,3,32]{4,3,2,0,1:T(4,128)(2,1)}, bf16[1,64,128,3,32]{4,3,2,0,1:T(4,128)(2,1)S(1)}) fusion(bf16[2,64,128,3,32]{4,3,2,0,1:T(4,128)(2,1)} %bitcast.215), kind=kLoop, calls=%fused_computation.144.clone.1 | loop fusion | bytes 6291456 | tf_op jit(solution)/shard_map/while/body/eval_jaxpr/slice | solution.py:109
  531.4 6.4 fusion.118
  537.7 10.4 %fusion.119 = bf16[1,8,128,3,32]{2,4,3,1,0:T(8,128)(2,1)S(1)} fusion(f32[8,3,128,1024]{3,2,1,0:T(8,128)} %get-tuple-element.414, f32[8,3,128]{2,1,0:T(4,128)S(1)} %get-tuple-element.415, f32[8,1024]{1,0:T(8,128)S(1)} %compare_convert_fusion.4, bf16[8,1024,3,32]{3,2,1,0:T(4,128)(2,1)} %bitcast.219), kind=kOutput, calls=%fused_computation.11.clone.1 | convolution fusion | flops 214007808 | bytes 14397440 | tf_op jit(solution)/shard_map/while/body/eval_jaxpr/ghqk,gkhd->gqhd/dot_general | solution.py:108
  550.3 9.8 %all_to_all.35 = bf16[4,512,96]{1,2,0:T(8,128)(2,1)S(1)} all-to-all(bf16[4,512,96]{1,2,0:T(8,128)(2,1)S(1)} %copy.67), channel_id=1, replica_groups=mesh['slab'=8,'head'=4] {'head'}, dimensions={0} | all-to-all | bytes 786432 | tf_op jit(solution)/shard_map/all_to_all | solution.py:116
  565.7 39.1 %psum.23 = f32[384]{0:T(512)} all-reduce(f32[384]{0:T(512)S(1)} %get-tuple-element.271), channel_id=1, replica_groups=mesh['slab'=8,'head'=4] {'slab','head'}, use_global_device_ids=true, to_apply=%region_18.19 | all-reduce | flops 384 | bytes 3072 | tf_op jit(solution)/shard_map/psum | solution.py:188
  604.8 2.1 fusion.58
  606.8 81.8 %all-reduce.5.cloned.1.call-done = f32[384,384]{1,0:T(8,128)} async-done(((f32[384,384]{1,0:T(8,128)}), f32[384,384]{1,0:T(8,128)}) %all-reduce.5.cloned.1.call-update) | async-done | bytes 589840 | tf_op jit(solution)/shard_map/psum | solution.py:188
  (156 shorter events, 34.9 us)
Async XLA Ops:
  7.2 26.9 %copy-start = (bf16[3,384,384]{2,1,0:T(8,128)(2,1)S(1)}, bf16[3,384,384]{2,1,0:T(8,128)(2,1)}, u32[]{:S(2)}) copy-start(bf16[3,384,384]{2,1,0:T(8,128)(2,1)} %param.21) | copy-start | bytes 2654212
  7.2 26.8 %all-gather.2.cloned.1.call-start = ((), (), s32[]{:S(2)}) async-start(), calls=%async_computation.3 | async-start | bytes 1966080 | tf_op jit(solution)/shard_map/all_gather | solution.py:82
  9.0 0.6 copy-start.26
  11.5 32.3 %copy-start.4 = (bf16[512,384]{1,0:T(8,128)(2,1)S(1)}, bf16[512,384]{1,0:T(8,128)(2,1)}, u32[]{:S(2)}) copy-start(bf16[512,384]{1,0:T(8,128)(2,1)} %param.23) | copy-start | bytes 1179652
  11.5 32.3 %copy-start.11 = (bf16[384,384]{1,0:T(8,128)(2,1)S(1)}, bf16[384,384]{1,0:T(8,128)(2,1)}, u32[]{:S(2)}) copy-start(bf16[384,384]{1,0:T(8,128)(2,1)} %param.22) | copy-start | bytes 884740
  36.5 1.5 copy-start.2
  36.5 12.0 %copy-start.30 = (s32[16,8]{0,1:T(8,128)S(1)}, s32[16,8]{0,1:T(8,128)}, u32[]{:S(2)}) copy-start(s32[16,8]{0,1:T(8,128)} %param.24) | copy-start | bytes 1540
  36.5 12.1 %copy-start.31 = (s32[16]{0:T(128)S(1)}, s32[16]{0:T(128)}, u32[]{:S(2)}) copy-start(s32[16]{0:T(128)} %param.25) | copy-start | bytes 196
  36.7 8.3 %copy-start.6 = (f32[1,2048,96]{1,2,0:T(8,128)}, f32[1,2048,96]{1,2,0:T(8,128)S(1)}, u32[]{:S(2)}) copy-start(f32[1,2048,96]{1,2,0:T(8,128)S(1)} %get-tuple-element.316) | copy-start | bytes 2359300
  36.7 8.3 %copy-start.8 = (f32[1,2048,96]{1,2,0:T(8,128)}, f32[1,2048,96]{1,2,0:T(8,128)S(1)}, u32[]{:S(2)}) copy-start(f32[1,2048,96]{1,2,0:T(8,128)S(1)} %get-tuple-element.315) | copy-start | bytes 2359300
  36.9 0.9 copy-start.23
  37.0 1.0 copy-start.25
  37.1 7.9 %copy-start.19 = (f32[2048,3]{0,1:T(4,128)}, f32[2048,3]{0,1:T(4,128)S(1)}, u32[]{:S(2)}) copy-start(f32[2048,3]{0,1:T(4,128)S(1)} %get-tuple-element.321) | copy-start | bytes 73732
  37.1 7.9 %copy-start.21 = (f32[2048,3]{0,1:T(4,128)}, f32[2048,3]{0,1:T(4,128)S(1)}, u32[]{:S(2)}) copy-start(f32[2048,3]{0,1:T(4,128)S(1)} %get-tuple-element.322) | copy-start | bytes 73732
  39.1 35.8 %collective-permute-start = (bf16[2,2048,96]{1,2,0:T(8,128)(2,1)}, bf16[2,2048,96]{1,2,0:T(8,128)(2,1)}, u32[]{:S(2)}, u32[]{:S(2)}) collective-permute-start(bf16[2,2048,96]{1,2,0:T(8,128)(2,1)} %pad_maximum_fusion.2), channel_id=1, source_target_pairs={{0,4},{4,8},{8,12},{12,16},{16,20},{20,24},{24,28},{28,0},{1,5},{5... | collective-permute-start | bytes 2359304 | tf_op jit(solution)/shard_map/ppermute | solution.py:24
  40.6 36.6 %collective-permute-start.1 = (bf16[2,2048,96]{1,2,0:T(8,128)(2,1)}, bf16[2,2048,96]{1,2,0:T(8,128)(2,1)}, u32[]{:S(2)}, u32[]{:S(2)}) collective-permute-start(bf16[2,2048,96]{1,2,0:T(8,128)(2,1)} %pad_maximum_fusion.2), channel_id=1, source_target_pairs={{4,0},{8,4},{12,8},{16,12},{20,16},{24,20},{28,24},{0,28},{5,1},{9... | collective-permute-start | bytes 2359304 | tf_op jit(solution)/shard_map/ppermute | solution.py:25
  45.0 10.9 %all-to-all-start.1 = ((bf16[512,4,96]{0,2,1:T(8,128)(2,1)}), bf16[512,4,96]{0,2,1:T(8,128)(2,1)S(1)}, u32[]{:S(2)}, u32[]{:S(2)}) async-start(bf16[512,4,96]{0,2,1:T(8,128)(2,1)} %bitcast.28), calls=%async_computation.1 | async-start | bytes 786432 | tf_op jit(solution)/shard_map/all_to_all | solution.py:124
  48.5 514.1 %all-reduce.3.cloned.1.call-start = ((), (), s32[]{:S(2)}) async-start(), calls=%async_computation.5 | async-start | bytes 442368 | tf_op jit(solution)/shard_map/psum | solution.py:186
  96.8 280.6 %copy-start.24 = (f32[2048,3]{0,1:T(4,128)S(1)}, f32[2048,3]{0,1:T(4,128)}, u32[]{:S(2)}) copy-start(f32[2048,3]{0,1:T(4,128)} %copy-done.23) | copy-start | bytes 73732
  158.5 6.6 copy-start.1
  177.5 9.8 %copy-start.15 = (bf16[2,8,128,3,32]{2,4,3,1,0:T(8,128)(2,1)S(1)}, bf16[2,8,128,3,32]{2,4,3,1,0:T(8,128)(2,1)}, u32[]{:S(2)}) copy-start(bf16[2,8,128,3,32]{2,4,3,1,0:T(8,128)(2,1)} %get-tuple-element.463) | copy-start | bytes 1179652 | tf_op jit(solution)/shard_map/while
  189.6 1.0 copy-start.16
  286.6 6.6 copy-start.1
  305.6 9.8 %copy-start.15 = (bf16[2,8,128,3,32]{2,4,3,1,0:T(8,128)(2,1)S(1)}, bf16[2,8,128,3,32]{2,4,3,1,0:T(8,128)(2,1)}, u32[]{:S(2)}) copy-start(bf16[2,8,128,3,32]{2,4,3,1,0:T(8,128)(2,1)} %get-tuple-element.463) | copy-start | bytes 1179652 | tf_op jit(solution)/shard_map/while
  317.7 1.0 copy-start.16
  367.5 14.0 %copy-start.9 = (f32[1,2048,96]{1,2,0:T(8,128)S(1)}, f32[1,2048,96]{1,2,0:T(8,128)}, u32[]{:S(2)}) copy-start(f32[1,2048,96]{1,2,0:T(8,128)} %copy-done.8) | copy-start | bytes 2359300
  367.5 14.0 %copy-start.20 = (f32[2048,3]{0,1:T(4,128)S(1)}, f32[2048,3]{0,1:T(4,128)}, u32[]{:S(2)}) copy-start(f32[2048,3]{0,1:T(4,128)} %copy-done.19) | copy-start | bytes 73732
  370.2 55.3 %collective-permute-start.3 = (f32[2,16,128,3,32]{2,4,3,1,0:T(8,128)}, f32[2,16,128,3,32]{2,4,3,1,0:T(8,128)}, u32[]{:S(2)}, u32[]{:S(2)}) collective-permute-start(f32[2,16,128,3,32]{2,4,3,1,0:T(8,128)} %slice.135), channel_id=1, source_target_pairs={{0,4},{4,8},{8,12},{12,16},{16,20},{20,24},{24,28},{28,0},{1,5},{5... | collective-permute-start | bytes 4718600 | tf_op jit(solution)/shard_map/ppermute | solution.py:33
  372.8 52.7 %collective-permute-start.2 = (bf16[2,16,128,3,32]{2,4,3,1,0:T(8,128)(2,1)}, bf16[2,16,128,3,32]{2,4,3,1,0:T(8,128)(2,1)}, u32[]{:S(2)}, u32[]{:S(2)}) collective-permute-start(bf16[2,16,128,3,32]{2,4,3,1,0:T(8,128)(2,1)} %slice.163), channel_id=1, source_target_pairs={{0,28},{4,0},{8,4},{12,8},{16,12},{20,16},{24,20},{28,24},{1,29},{... | collective-permute-start | bytes 2359304 | tf_op jit(solution)/shard_map/ppermute | solution.py:33
  383.6 47.8 %copy-start.7 = (f32[1,2048,96]{1,2,0:T(8,128)S(1)}, f32[1,2048,96]{1,2,0:T(8,128)}, u32[]{:S(2)}) copy-start(f32[1,2048,96]{1,2,0:T(8,128)} %copy-done.6) | copy-start | bytes 2359300
  383.6 47.8 %copy-start.22 = (f32[2048,3]{0,1:T(4,128)S(1)}, f32[2048,3]{0,1:T(4,128)}, u32[]{:S(2)}) copy-start(f32[2048,3]{0,1:T(4,128)} %copy-done.21) | copy-start | bytes 73732
  433.5 5.9 copy-start.10
  435.7 6.3 copy-start.13
  438.6 0.7 copy-start.17
  438.6 0.9 copy-start.18
  442.0 122.3 %reduce-scatter.2.cloned.1.call-start = ((), (), s32[]{:S(2)}) async-start(), calls=%async_computation.4 | async-start | bytes 1966080 | tf_op jit(solution)/shard_map/reduce_scatter | solution.py:177
  445.6 243.0 %all-reduce.5.cloned.1.call-start = ((), (), s32[]{:S(2)}) async-start(), calls=%async_computation.6 | async-start | bytes 1179648 | tf_op jit(solution)/shard_map/psum | solution.py:188
  445.7 114.4 %copy-start.5 = (bf16[512,384]{1,0:T(8,128)(2,1)S(1)}, bf16[512,384]{1,0:T(8,128)(2,1)}, u32[]{:S(2)}) copy-start(bf16[512,384]{1,0:T(8,128)(2,1)} %param.23) | copy-start | bytes 1179652
  445.7 115.6 %copy-start.3 = (bf16[512,384]{1,0:T(8,128)(2,1)S(1)}, bf16[512,384]{1,0:T(8,128)(2,1)}, u32[]{:S(2)}) copy-start(bf16[512,384]{1,0:T(8,128)(2,1)} %param.19) | copy-start | bytes 1179652
  445.7 115.6 %copy-start.12 = (bf16[384,384]{1,0:T(8,128)(2,1)S(1)}, bf16[384,384]{1,0:T(8,128)(2,1)}, u32[]{:S(2)}) copy-start(bf16[384,384]{1,0:T(8,128)(2,1)} %param.22) | copy-start | bytes 884740
  548.3 0.7 copy-start.14
  549.0 15.3 %copy-start.27 = (f32[512]{0:T(512)S(1)}, f32[512]{0:T(512)}, u32[]{:S(2)}) copy-start(f32[512]{0:T(512)} %copy-done.26) | copy-start | bytes 6148
  549.0 15.3 %copy-start.28 = (f32[384]{0:T(512)S(1)}, f32[384]{0:T(512)}, u32[]{:S(2)}) copy-start(f32[384]{0:T(512)} %param.20) | copy-start | bytes 4612
  549.0 55.7 %copy-start.29 = (f32[512]{0:T(512)S(1)}, f32[512]{0:T(512)}, u32[]{:S(2)}) copy-start(f32[512]{0:T(512)} %get-tuple-element.319) | copy-start | bytes 6148
Sparse Core Ops, SparseCore 0:
  11.6 22.3 all-gather.1
  442.1 68.5 all-reduce.2
  513.4 27.4 reduce-scatter.1
  562.6 125.9 all-reduce.4
where the time goes:
time: 704 us; the launch traced here: 697 us
  local copies, waits for them, and re-layouts  247 us (35%)
  waiting for transfers between devices  174 us (25%)
  matrix products  102 us (14%)
  other arithmetic  83.2 us (12%)
  blocking collectives  48.9 us (7%)
  loops' own time  14.8 us (2%)
  between operations  14.3 us (2%)
  starting transfers between devices  13.1 us (2%)
    gather x4, local copies, waits for them, and re-layouts, fetch(): both = key_blocks[:, lookup_rows.reshape(-1)]  83.7 us
    psum x1, waiting for transfers between devices, local(): d_w_out, d_gain = lax.psum((d_out_part, d_gain_part), ('slab', 'head'))  81.8 us
    ppermute x2, waiting for transfers between devices, passed_along(): return lax.ppermute(value, axis, pairs)  41.9 us
    psum x1, blocking collectives, local(): d_w_out, d_gain = lax.psum((d_out_part, d_gain_part), ('slab', 'head'))  39.1 us
    scatter-add x2, other arithmetic, backward_group(): grad_buffer = grad_buffer.at[:, lookup_rows.reshape(-1)].add(stacked)  33.1 us
    slice x2, local copies, waits for them, and re-layouts, backward_group(): both[1]  32 us
    another operation x6, local copies, waits for them, and re-layouts, backward_group(): jnp.stack([d_keys, d_values])  30.9 us
    slice x2, local copies, waits for them, and re-layouts, attend(): both[1]  26.4 us
  transfers between devices with their start and end apart: 9, of which 6 were waited for; matrix products, arithmetic and copies ran while one was open for 18% of the time, Pallas kernels for 0%

commit v1 on v0

v1 whole, which is shorter than its diff:
```python
import functools
import math

import jax
import jax.numpy as jnp
from jax import lax
from jax.experimental import pallas as pl
from jax.experimental.pallas import tpu as pltpu
from jax.sharding import PartitionSpec as P

HEADS = 12
BLK = 128
REACH = 16
MESH = pl.DeviceIdType.MESH
F32, BF16 = jnp.float32, jnp.bfloat16

SCORE_SCALE = 10.0
LOG2E = 1.0 / math.log(2.0)
norm_eps = 1e-06


def dot(a, b):
    return jnp.dot(a, b, preferred_element_type=F32)


def attention_kernel(
    n_heads, hd, n_slots, lookup_ref, counts_ref, q_ref, do_ref, low_ref, own_ref, high_ref,
    att_ref, dq_ref, g_low_ref, g_own_ref, g_high_ref,
    kv_t, k_n, v_n, dk_acc, dv_acc, e_s, ds_s,
):
    cols = n_heads * hd
    wide = n_heads * BLK
    pieces = ((low_ref, g_low_ref), (own_ref, g_own_ref), (high_ref, g_high_ref))

    first = 0
    for ref, _ in pieces:
        blocks = ref.shape[1] // BLK

        @pl.loop(0, blocks)
        def _(i, ref=ref, first=first):
            at = pl.ds(pl.multiple_of(i * BLK, BLK), BLK)
            both = ref[:, at]
            kv_t[first + i] = both
            k_n[first + i] = both[:cols].T
            v_n[first + i] = both[cols:].T
            zero = jnp.zeros((BLK, cols), F32)
            dk_acc[first + i] = zero
            dv_acc[first + i] = zero

        first += blocks

    def diagonal(parts):
        rows = []
        for h in range(n_heads):
            zero = jnp.zeros((hd, BLK), BF16)
            rows.append(
                jnp.concatenate([parts[h] if g == h else zero for g in range(n_heads)], axis=1)
            )
        return jnp.concatenate(rows, axis=0)

    def of_head(value, h):
        return value[h * hd : (h + 1) * hd, h * BLK : (h + 1) * BLK]

    @pl.loop(0, q_ref.shape[1] // BLK)
    def _(b):
        at = pl.ds(pl.multiple_of(b * BLK, BLK), BLK)
        q_t = q_ref[:, at]
        do_t = do_ref[:, at]
        slots = [lookup_ref[b, j] for j in range(n_slots)]
        count = counts_ref[b]
        q_diag = diagonal([q_t[h * hd : (h + 1) * hd] for h in range(n_heads)])
        total = jnp.zeros((1, wide), F32)
        for j in range(n_slots):
            raised = jnp.exp2(dot(k_n[slots[j]], q_diag))
            raised = raised * jnp.where(j < count, 1.0, 0.0)
            total = total + jnp.sum(raised, axis=0, keepdims=True)
            e_s[j * BLK : (j + 1) * BLK, :] = raised.astype(BF16)
        values_t = jnp.concatenate([kv_t[s][cols:] for s in slots], axis=1)
        keys_t = jnp.concatenate([kv_t[s][:cols] for s in slots], axis=1)
        out = dot(values_t, e_s[...])
        share = 1.0 / total
        att, scaled, inner = [], [], []
        for h in range(n_heads):
            share_h = share[:, h * BLK : (h + 1) * BLK]
            att_h = of_head(out, h) * share_h
            do_h = do_t[h * hd : (h + 1) * hd].astype(F32) * share_h
            att.append(att_h)
            scaled.append(do_h.astype(BF16))
            inner.append(jnp.sum(att_h * do_h, axis=0, keepdims=True))
        att_ref[:, at] = jnp.concatenate(att, axis=0).astype(BF16)
        inner = jnp.concatenate(inner, axis=1)
        do_diag = diagonal(scaled)
        q_rows = q_diag.T
        do_rows = do_diag.T
        for j in range(n_slots):
            rows = slice(j * BLK, (j + 1) * BLK)
            e = e_s[rows, :]
            d = e.astype(F32) * (dot(v_n[slots[j]], do_diag) - inner)
            d = d.astype(BF16)
            ds_s[rows, :] = d
            dk_acc[slots[j]] += dot(d, q_rows)
            dv_acc[slots[j]] += dot(e, do_rows)
        dq = dot(keys_t, ds_s[...])
        dq = jnp.concatenate([of_head(dq, h) for h in range(n_heads)], axis=0)
        dq_ref[:, at] = (dq * SCORE_SCALE).astype(dq_ref.dtype)

    first = 0
    for ref, g_ref in pieces:
        blocks = ref.shape[1] // BLK

        @pl.loop(0, blocks)
        def _(i, g_ref=g_ref, first=first):
            at = pl.ds(pl.multiple_of(i * BLK, BLK), BLK)
            g_ref[:cols, at] = (dk_acc[first + i] * math.log(2.0)).T.astype(g_ref.dtype)
            g_ref[cols:, at] = dv_acc[first + i].T.astype(g_ref.dtype)

        first += blocks


def attention(lookup, counts, q_t, do_t, low, own, high, hd=32):
    cols, rows = q_t.shape
    n_heads = cols // hd
    n_slots = lookup.shape[1]
    ext = (low.shape[1] + own.shape[1] + high.shape[1]) // BLK
    smem = pl.BlockSpec(memory_space=pltpu.SMEM)
    vmem = pl.BlockSpec(memory_space=pltpu.VMEM)
    shape = jax.ShapeDtypeStruct
    return pl.pallas_call(
        functools.partial(attention_kernel, n_heads, hd, n_slots),
        out_shape=(
            shape((cols, rows), BF16),
            shape((cols, rows), BF16),
            shape(low.shape, BF16),
            shape(own.shape, F32),
            shape(high.shape, BF16),
        ),
        in_specs=[smem, smem] + [vmem] * 5,
        out_specs=(vmem,) * 5,
        scratch_shapes=[
            pltpu.VMEM((ext, 2 * cols, BLK), BF16),
            pltpu.VMEM((ext, BLK, cols), BF16),
            pltpu.VMEM((ext, BLK, cols), BF16),
            pltpu.VMEM((ext, BLK, cols), F32),
            pltpu.VMEM((ext, BLK, cols), F32),
            pltpu.VMEM((n_slots * BLK, n_heads * BLK), BF16),
            pltpu.VMEM((n_slots * BLK, n_heads * BLK), BF16),
        ],
        compiler_params=pltpu.CompilerParams(vmem_limit_bytes=52 * 1024 * 1024),
    )(lookup, counts, q_t, do_t, low, own, high)


def sums_kernel(
    n_slab, n_head, qkv_ref, out_part_ref, w_ref, gain_ref,
    d_qkv_ref, d_out_ref, d_gain_ref,
    heads_in, full, slabs_in, chunk, done_out, gain_part, gains_in,
    send_a, recv_a, send_b, recv_b, send_c, recv_c, send_d, recv_d, send_e, recv_e,
):
    slab, head = lax.axis_index("slab"), lax.axis_index("head")
    rows_q = qkv_ref.shape[0]
    rows_o = out_part_ref.shape[0] // n_head
    step = chunk.shape[0]

    def other_heads():
        return [(k, lax.rem(head + k, n_head)) for k in range(1, n_head)]

    def other_slabs():
        return [(k, lax.rem(slab + k, n_slab)) for k in range(1, n_slab)]

    barrier = pltpu.get_barrier_semaphore()
    for _, h in other_heads():
        pl.semaphore_signal(barrier, inc=1, device_id=(slab, h), device_id_type=MESH)
    for _, s in other_slabs():
        pl.semaphore_signal(barrier, inc=1, device_id=(s, head), device_id_type=MESH)
    pl.semaphore_wait(barrier, n_head + n_slab - 2)

    def send(src, dst, send_sem, recv_sem, target):
        copy = pltpu.make_async_remote_copy(
            src_ref=src, dst_ref=dst, send_sem=send_sem, recv_sem=recv_sem,
            device_id=target, device_id_type=MESH,
        )
        copy.start()
        return copy

    pending = []
    for k, h in other_heads():
        rows = pl.ds(pl.multiple_of(h * rows_o, 16), rows_o)
        pending.append(
            send(out_part_ref.at[rows], heads_in.at[k], send_a.at[k], recv_a.at[k], (slab, h))
        )
    full[:rows_q, :] = qkv_ref[...]
    if full.shape[0] > rows_q + rows_o:
        full[rows_q + rows_o :, :] = jnp.zeros(
            (full.shape[0] - rows_q - rows_o, full.shape[1]), BF16
        )
    mine = pl.ds(pl.multiple_of(head * rows_o, 16), rows_o)
    total = out_part_ref[mine, :].astype(F32)
    for k in range(1, n_head):
        pending[k - 1].wait()
        total += heads_in[k].astype(F32)
    full[rows_q : rows_q + rows_o, :] = total.astype(BF16)

    pending = []
    for k, s in other_slabs():
        rows = pl.ds(pl.multiple_of(s * step, 16), step)
        pending.append(send(full.at[rows], slabs_in.at[k], send_b.at[k], recv_b.at[k], (s, head)))
    mine = pl.ds(pl.multiple_of(slab * step, 16), step)
    total = full[mine, :].astype(F32)
    for k in range(1, n_slab):
        pending[k - 1].wait()
        total += slabs_in[k].astype(F32)
    chunk[...] = total.astype(BF16)
    pending = []
    for k, s in other_slabs():
        pending.append(send(chunk, done_out.at[mine], send_c.at[k], recv_c.at[k], (s, head)))
    done_out[mine, :] = chunk[...]
    for copy in pending:
        copy.wait()

    mine = pl.ds(pl.multiple_of(head * rows_o, 16), rows_o)
    own = done_out.at[pl.ds(rows_q, rows_o)]
    pending = []
    for k, h in other_heads():
        pending.append(send(own, heads_in.at[n_head + k], send_d.at[k], recv_d.at[k], (slab, h)))
    summed = done_out[:rows_q, :].astype(F32)
    part = jnp.sum(summed * w_ref[...].astype(F32), axis=0, keepdims=True) / gain_ref[...]
    gain_part[...] = jnp.broadcast_to(part, gain_part.shape)
    for k, h in other_heads():
        pending.append(send(gain_part, gains_in.at[k], send_e.at[k], recv_e.at[k], (slab, h)))
    d_qkv_ref[...] = summed
    d_out_ref[mine, :] = done_out[rows_q : rows_q + rows_o, :].astype(F32)
    for copy in pending:
        copy.wait()
    total = gain_part[...]
    for k in range(1, n_head):
        source = lax.rem(head + n_head - k, n_head)
        rows = pl.ds(pl.multiple_of(source * rows_o, 16), rows_o)
        d_out_ref[rows, :] = heads_in[n_head + k].astype(F32)
        total += gains_in[k]
    d_gain_ref[...] = total


def grad_sums(qkv_part, out_part, w_t, gain):
    n_slab, n_head = lax.axis_size("slab"), lax.axis_size("head")
    rows_q, width = qkv_part.shape
    rows_o = out_part.shape[0] // n_head
    step = -(-(rows_q + rows_o) // (16 * n_slab)) * 16
    vmem = pl.BlockSpec(memory_space=pltpu.VMEM)
    shape = jax.ShapeDtypeStruct
    dma = pltpu.SemaphoreType.DMA
    return pl.pallas_call(
        functools.partial(sums_kernel, n_slab, n_head),
        out_shape=(
            shape((rows_q, width), F32),
            shape(out_part.shape, F32),
            shape((8, width), F32),
        ),
        in_specs=[vmem] * 4,
        out_specs=(vmem,) * 3,
        scratch_shapes=[
            pltpu.VMEM((2 * n_head, rows_o, width), BF16),
            pltpu.VMEM((n_slab * step, width), BF16),
            pltpu.VMEM((n_slab, step, width), BF16),
            pltpu.VMEM((step, width), BF16),
            pltpu.VMEM((n_slab * step, width), BF16),
            pltpu.VMEM((8, width), F32),
            pltpu.VMEM((n_head, 8, width), F32),
        ]
        + [dma((n,)) for n in (n_head, n_head, n_slab, n_slab, n_slab, n_slab)]
        + [dma((n_head,))] * 4,
        compiler_params=pltpu.CompilerParams(
            collective_id=0, has_side_effects=True, vmem_limit_bytes=32 * 1024 * 1024
        ),
        cost_estimate=pl.CostEstimate(flops=0, bytes_accessed=30_000_000, transcendentals=0),
    )(qkv_part, out_part, w_t, gain)


def shifted(value, steps):
    size = lax.axis_size("slab")
    return lax.ppermute(value, "slab", [(i, (i + steps) % size) for i in range(size)])


def local(tokens, norm_gain, w_qkv, w_out, cotangent, neighbours, counts):
    width = tokens.shape[1]
    hd = width // HEADS
    n_head, n_slab = lax.axis_size("head"), lax.axis_size("slab")
    cols = width // n_head
    here = HEADS // n_head
    head_index, slab_index = lax.axis_index("head"), lax.axis_index("slab")
    slab_blocks, n_slots = neighbours.shape
    slab_rows = slab_blocks * BLK
    halo = REACH * BLK
    tok = tokens.astype(F32)
    inverse = lax.rsqrt(jnp.mean(tok * tok, -1, keepdims=True) + norm_eps)
    normed = (tok * inverse * norm_gain).astype(BF16)
    gathered = lax.all_gather(normed, "head", axis=0, tiled=True)
    w_here = lax.dynamic_slice_in_dim(w_qkv, head_index * cols, cols, 2)
    w_t = w_here.transpose(0, 2, 1).reshape(3 * cols, width)

    d_attended = lax.dot_general(
        w_out, cotangent, (((1,), (1,)), ((), ())), preferred_element_type=F32
    ).astype(BF16)
    d_heads = lax.all_to_all(d_attended, "head", split_axis=0, concat_axis=1, tiled=True)

    projected = lax.dot_general(
        w_t, gathered, (((1,), (1,)), ((), ())), preferred_element_type=F32
    )
    by_head = projected[: 2 * cols].reshape(2, here, hd, slab_rows)
    length = jnp.sqrt(jnp.sum(by_head * by_head, 2, keepdims=True))
    floor = 0.7 * math.sqrt(hd)
    divisor = jnp.maximum(length, floor)
    unit = by_head / divisor
    q_t = (unit[0] * (SCORE_SCALE * LOG2E)).reshape(cols, slab_rows).astype(BF16)
    kv_t = jnp.concatenate(
        [unit[1].reshape(cols, slab_rows).astype(BF16), projected[2 * cols :].astype(BF16)], 0
    )
    low = shifted(kv_t[:, slab_rows - halo :], 1)
    high = shifted(kv_t[:, :halo], -1)
    lookup = (neighbours - slab_index * slab_blocks + REACH) % (slab_blocks * n_slab)
    attended_t, dq_t, g_low, g_own, g_high = attention(
        lookup, counts, q_t, d_heads, low, kv_t, high, hd
    )
    from_above = shifted(g_low, -1).astype(F32)
    from_below = shifted(g_high, 1).astype(F32)

    attended = lax.all_to_all(attended_t, "head", split_axis=1, concat_axis=0, tiled=True)
    output = (
        tok
        + lax.dot_general(attended, w_out, (((0,), (0,)), ((), ())), preferred_element_type=F32)
    ).astype(BF16)
    d_out_part = dot(attended, cotangent)

    if slab_rows == halo:
        g_kv = g_own + from_above + from_below
    else:
        g_kv = g_own.at[:, slab_rows - halo :].add(from_above).at[:, :halo].add(from_below)
    along = jnp.stack([dq_t.astype(F32), g_kv[:cols]]).reshape(2, here, hd, slab_rows)
    inner = jnp.sum(unit * along, 2, keepdims=True)
    d_qk = (along - jnp.where(length > floor, unit * inner, 0.0)) / divisor
    d_qkv = jnp.concatenate(
        [d_qk.reshape(2 * cols, slab_rows).astype(BF16), g_kv[cols:].astype(BF16)], 0
    )
    d_normed = lax.psum_scatter(
        lax.dot_general(
            d_qkv, w_t, (((0,), (0,)), ((), ())), preferred_element_type=F32
        ).astype(BF16),
        "head",
        scatter_dimension=0,
        tiled=True,
    ).astype(F32)
    d_qkv_part = dot(d_qkv, gathered).astype(BF16)
    d_w, d_w_out, d_gain = grad_sums(
        d_qkv_part, d_out_part.astype(BF16), w_t, norm_gain.reshape(1, width)
    )
    d_w_qkv = d_w.reshape(3, cols, width).transpose(0, 2, 1)
    scaled = d_normed * norm_gain
    d_tokens = (
        cotangent.astype(F32)
        + inverse * scaled
        - tok * inverse**3 * jnp.mean(scaled * tok, -1, keepdims=True)
    )
    return (output, d_tokens.astype(BF16), d_w_qkv, d_w_out, d_gain[0])


def solution(mesh):
    placed = (
        P(("slab", "head"), None),
        P(),
        P(),
        P(),
        P(("slab", "head"), None),
        P("slab", None),
        P("slab"),
    )
    return jax.shard_map(
        local,
        mesh=mesh,
        in_specs=placed,
        out_specs=(
            P(("slab", "head"), None),
            P(("slab", "head"), None),
            P(None, None, "head"),
            P(),
            P(),
        ),
        check_vma=False,
    )
```

time: 704 us -> 228 us (0.32)
  local copies, waits for them, and re-layouts: 247 us -> 8.05 us
  matrix products: 102 us -> 9.22 us
  waiting for transfers between devices: 174 us -> 90 us
  Pallas kernels: 0 us -> 76.5 us
  other arithmetic: 83.2 us -> 12.5 us
  blocking collectives: 48.9 us -> 0 us
  loops' own time: 14.8 us -> 0 us
    dot_general x20 -> x6, matrix products: 102 us -> 9.22 us  [the longest x1 2.36 us: local(): lax.dot_general(d_qkv, w_t, (((0,), (0,)), ((), ())), preferred_element_t...]
    gather x4 -> x0, local copies, waits for them, and re-layouts: 83.7 us -> none  [fetch(): both = key_blocks[:, lookup_rows.reshape(-1)]]
    psum x2 -> x0, waiting for transfers between devices: 81.8 us -> none  [the longest x1 81.8 us: local(): d_w_out, d_gain = lax.psum((d_out_part, d_gain_part), ('slab', 'head'))]
    pallas_call x0 -> x2, Pallas kernels: none -> 76.5 us  [the longest x1 47.2 us: attention(): pl.pallas_call(functools.partial(attention_kernel, n_heads, hd, n_slots),...]
    slice x10 -> x6, local copies, waits for them, and re-layouts: 66 us -> 0.92 us  [the longest x1 0.6 us: local(): return (output, d_tokens.astype(BF16), d_w_qkv, d_w_out, d_gain[0])]
    psum x1 -> x0, blocking collectives: 39.1 us -> none  [local(): d_w_out, d_gain = lax.psum((d_out_part, d_gain_part), ('slab', 'head'))]
    scatter-add x2 -> x0, other arithmetic: 33.1 us -> none  [backward_group(): grad_buffer = grad_buffer.at[:, lookup_rows.reshape(-1)].add(stacked)]
    another operation x6 -> x0, local copies, waits for them, and re-layouts: 30.9 us -> none  [backward_group(): jnp.stack([d_keys, d_values])]
  transfers between devices with their start and end apart: 9 -> 8, of which waited for: 6 -> 6; matrix products, arithmetic and copies ran while one was open for 18% -> 3% of each run, Pallas kernels for 0% -> 13%
where the time goes in v1:
time: 228 us; the launch traced here: 227 us
  waiting for transfers between devices  90 us (39%)
  Pallas kernels  76.5 us (34%)
  starting transfers between devices  16 us (7%)
  between operations  14.4 us (6%)
  other arithmetic  12.5 us (5%)
  matrix products  9.22 us (4%)
  local copies, waits for them, and re-layouts  8.05 us (4%)
    ppermute x4, waiting for transfers between devices, shifted(): lax.ppermute(value, 'slab', [(i, (i + steps) % size) for i in range(size)])  53.1 us
    pallas_call x1, Pallas kernels, attention(): pl.pallas_call(functools.partial(attention_kernel, n_heads, hd, n_slots),...  47.2 us
    pallas_call x1, Pallas kernels, grad_sums(): pl.pallas_call(functools.partial(sums_kernel, n_slab, n_head), out_shape=...  29.4 us
    all_gather x1, waiting for transfers between devices, local(): gathered = lax.all_gather(normed, 'head', axis=0, tiled=True)  22.1 us
    ppermute x4, starting transfers between devices, shifted(): lax.ppermute(value, 'slab', [(i, (i + steps) % size) for i in range(size)])  8.74 us
    all_to_all x1, waiting for transfers between devices, local(): lax.all_to_all(attended_t, 'head', split_axis=1, concat_axis=0, tiled=True)  7.39 us
    all_to_all x1, waiting for transfers between devices, local(): lax.all_to_all(d_attended, 'head', split_axis=0, concat_axis=1, tiled=True)  7.26 us
    unnamed x37, local copies, waits for them, and re-layouts  5.95 us
  transfers between devices with their start and end apart: 8, of which 6 were waited for; matrix products, arithmetic and copies ran while one was open for 3% of the time, Pallas kernels for 13%

profile of v1, /device:TPU:0, one launch (start us, length us, event | category | flops | bytes accessed | tf_op | source)
XLA Modules:
  0.0 226.7 jit_solution(3893239509987282332)
XLA Ops:
  7.2 0.0 copy-start
  7.2 0.0 all-gather.2.cloned.1.call-start
  7.2 1.2 fusion.7
  8.4 0.6 multiply_multiply_fusion
  9.0 1.9 fusion.9
  10.9 0.0 all-gather.2.cloned.1.call-update
  11.0 0.2 dynamic-slice_bitcast_fusion
  11.1 0.2 copy.20
  11.3 22.1 %all-gather.2.cloned.1.call-done = bf16[2048,384]{1,0:T(8,128)(2,1)} async-done(((bf16[512,384]{1,0:T(8,128)(2,1)}), bf16[2048,384]{1,0:T(8,128)(2,1)}) %all-gather.2.cloned.1.call-update) | async-done | bytes 1572880 | tf_op jit(solution)/shard_map/all_gather | solution.py:295
  33.5 2.2 fusion.18
  35.7 0.0 copy-start.2
  35.8 0.1 slice.31
  35.9 1.2 copy-done.2
  37.1 0.2 multiply_reduce_fusion.1
  37.4 0.0 copy-start.10
  37.4 0.6 copy-done.10
  38.0 0.2 broadcast_divide_fusion
  38.2 0.0 copy-start.5
  38.2 0.0 copy-start.7
  38.2 0.0 copy-start.16
  38.2 1.0 pad_maximum_fusion.2.own_ref
  39.2 4.2 %collective-permute-start.1 = (bf16[192,2048]{1,0:T(8,128)(2,1)}, bf16[192,2048]{1,0:T(8,128)(2,1)}, u32[]{:S(2)}, u32[]{:S(2)}) collective-permute-start(bf16[192,2048]{1,0:T(8,128)(2,1)} %pad_maximum_fusion.2.own_ref), channel_id=1, source_target_pairs={{0,28},{4,0},{8,4},{12,8},{16,12},{20,16},{24,20},{28,24},{1,29},{... | collective-permute-start | bytes 2359304 | tf_op jit(solution)/shard_map/ppermute | solution.py:279
  43.5 0.0 collective-permute-start
  43.5 1.1 convolution_convert_fusion.1
  44.6 3.6 %all-to-all-start = ((bf16[4,96,512]{2,1,0:T(8,128)(2,1)}), bf16[4,96,512]{2,1,0:T(8,128)(2,1)S(1)}, u32[]{:S(2)}, u32[]{:S(2)}) async-start(bf16[4,96,512]{2,1,0:T(8,128)(2,1)} %bitcast.71), calls=%async_computation | async-start | bytes 786432 | tf_op jit(solution)/shard_map/all_to_all | solution.py:302
  48.2 0.0 reduce-scatter.2.cloned.1.call-start
  48.3 0.1 copy.19
  48.4 7.3 %all-to-all-done = bf16[4,96,512]{2,1,0:T(8,128)(2,1)S(1)} async-done(((bf16[4,96,512]{2,1,0:T(8,128)(2,1)}), bf16[4,96,512]{2,1,0:T(8,128)(2,1)S(1)}, u32[]{:S(2)}, u32[]{:S(2)}) %all-to-all-start) | async-done | bytes 393248 | tf_op jit(solution)/shard_map/all_to_all | solution.py:302
  55.7 0.1 fusion.14
  55.7 20.3 %collective-permute-done.1.high_ref = bf16[192,2048]{1,0:T(8,128)(2,1)} collective-permute-done((bf16[192,2048]{1,0:T(8,128)(2,1)}, bf16[192,2048]{1,0:T(8,128)(2,1)}, u32[]{:S(2)}, u32[]{:S(2)}) %collective-permute-start.1) | collective-permute-done | bytes 786464 | tf_op jit(solution)/shard_map/ppermute | solution.py:279
  76.1 0.0 collective-permute-done.low_ref
  76.1 47.2 %shard_map.110 = (bf16[96,2048]{1,0:T(8,128)(2,1)S(1)}, bf16[96,2048]{1,0:T(8,128)(2,1)S(1)}, bf16[192,2048]{1,0:T(8,128)(2,1)}, f32[192,2048]{1,0:T(8,128)}, bf16[192,2048]{1,0:T(8,128)(2,1)}) custom-call(s32[16,8]{1,0:T(8,128)S(1)} %add_select_fusion.lookup_ref, s32[16]{0:T(128)S(1)} %copy-done.1, bf16[96,2048]{1,0:T(8,128)(2,1)S(1)} %bitcast.60, ...), custom_call_target="tpu_custom_call" | custom-call | tf_op jit(solution)/shard_map/pallas_call | solution.py:128
  123.2 4.5 %collective-permute-start.2 = (bf16[192,2048]{1,0:T(8,128)(2,1)}, bf16[192,2048]{1,0:T(8,128)(2,1)S(1)}, u32[]{:S(2)}, u32[]{:S(2)}) collective-permute-start(bf16[192,2048]{1,0:T(8,128)(2,1)} %get-tuple-element.16), channel_id=1, source_target_pairs={{0,28},{4,0},{8,4},{12,8},{16,12},{20,16},{24,20},{28,24},{1,29},{... | collective-permute-start | bytes 2359304 | tf_op jit(solution)/shard_map/ppermute | solution.py:279
  127.7 0.0 collective-permute-start.3
  127.7 0.1 sqrt_compare_fusion
  127.8 0.1 convert.13
  127.9 32.5 %collective-permute-done.2 = bf16[192,2048]{1,0:T(8,128)(2,1)S(1)} collective-permute-done((bf16[192,2048]{1,0:T(8,128)(2,1)}, bf16[192,2048]{1,0:T(8,128)(2,1)S(1)}, u32[]{:S(2)}, u32[]{:S(2)}) %collective-permute-start.2) | collective-permute-done | bytes 786464 | tf_op jit(solution)/shard_map/ppermute | solution.py:279
  160.4 0.3 collective-permute-done.3
  160.7 1.7 convert_add_fusion
  162.5 0.0 copy-start.12
  162.5 0.1 slice.35
  162.5 1.6 fusion
  164.1 0.0 copy-start.3
  164.1 0.1 pad_maximum_fusion
  164.2 1.5 copy-done.3
  165.8 0.5 fusion.5
  166.3 0.0 copy-done.12
  166.3 0.9 copy-done.9
  167.2 2.4 %convolution_convert_fusion = bf16[2048,384]{1,0:T(8,128)(2,1)} fusion(bf16[288,384]{1,0:T(8,128)(2,1)S(1)} %bitcast.57, bf16[96,2048]{1,0:T(8,128)(2,1)S(1)} %slice.45, bf16[192,2048]{1,0:T(8,128)(2,1)S(1)} %fusion.5), kind=kOutput, calls=%fused_computation.1 | convolution fusion | flops 456130560 | bytes 2973696 | tf_op jit(solution)/shard_map/dot_general | solution.py:343
  169.6 0.0 reduce-scatter.2.cloned.1.call-update
  169.6 0.0 copy-start.4
  169.6 0.0 copy-start.8
  169.6 0.8 copy.26
  170.4 3.6 %all-to-all-start.1 = ((bf16[96,4,512]{2,0,1:T(8,128)(2,1)}), bf16[96,4,512]{2,0,1:T(8,128)(2,1)S(1)}, u32[]{:S(2)}, u32[]{:S(2)}) async-start(bf16[96,4,512]{2,0,1:T(8,128)(2,1)} %bitcast.55), calls=%async_computation.1 | async-start | bytes 786432 | tf_op jit(solution)/shard_map/all_to_all | solution.py:325
  174.0 7.4 %all-to-all-done.1 = bf16[96,4,512]{2,0,1:T(8,128)(2,1)S(1)} async-done(((bf16[96,4,512]{2,0,1:T(8,128)(2,1)}), bf16[96,4,512]{2,0,1:T(8,128)(2,1)S(1)}, u32[]{:S(2)}, u32[]{:S(2)}) %all-to-all-start.1) | async-done | bytes 393248 | tf_op jit(solution)/shard_map/all_to_all | solution.py:325
  181.4 0.4 convolution_convert_fusion.2.out_part_ref
  181.8 1.2 fusion.6
  183.0 1.9 convolution_convert_fusion.3.qkv_ref
  185.0 29.4 %shard_map.111 = (f32[288,384]{1,0:T(8,128)S(1)}, f32[384,384]{1,0:T(8,128)S(1)}, f32[8,384]{1,0:T(8,128)S(1)}) custom-call(bf16[288,384]{1,0:T(8,128)(2,1)S(1)} %convolution_convert_fusion.3.qkv_ref, bf16[384,384]{1,0:T(8,128)(2,1)S(1)} %convolution_convert_fusion.2.out_part_ref, bf16[288,384]{1,0:T(8,128)(2,1)S(1)} %bitcast.58, ...), custom_call_target="tpu_custom_call" | custom-call | bytes 30000000 | tf_op jit(solution)/shard_map/pallas_call | solution.py:250
  214.3 0.6 slice_reduce_fusion
  214.9 1.2 fusion.13
  216.2 2.1 fusion.12
  218.3 0.8 copy.29
  219.0 0.8 copy.30
  (28 shorter events, 0.3 us)
Async XLA Ops:
  7.2 3.8 %copy-start = (bf16[3,384,384]{2,1,0:T(8,128)(2,1)S(1)}, bf16[3,384,384]{2,1,0:T(8,128)(2,1)}, u32[]{:S(2)}) copy-start(bf16[3,384,384]{2,1,0:T(8,128)(2,1)} %param.9) | copy-start | bytes 2654212
  7.2 26.3 %all-gather.2.cloned.1.call-start = ((), (), s32[]{:S(2)}) async-start(), calls=%async_computation.3 | async-start | bytes 1966080 | tf_op jit(solution)/shard_map/all_gather | solution.py:295
  35.7 1.4 copy-start.2
  37.4 0.6 copy-start.10
  38.2 5.3 %copy-start.5 = (bf16[512,384]{1,0:T(8,128)(2,1)S(1)}, bf16[512,384]{1,0:T(8,128)(2,1)}, u32[]{:S(2)}) copy-start(bf16[512,384]{1,0:T(8,128)(2,1)} %param.11) | copy-start | bytes 1179652
  38.2 5.3 %copy-start.7 = (bf16[384,384]{1,0:T(8,128)(2,1)S(1)}, bf16[384,384]{1,0:T(8,128)(2,1)}, u32[]{:S(2)}) copy-start(bf16[384,384]{1,0:T(8,128)(2,1)} %param.10) | copy-start | bytes 884740
  38.2 10.0 %copy-start.16 = (s32[16,8]{0,1:T(8,128)S(1)}, s32[16,8]{0,1:T(8,128)}, u32[]{:S(2)}) copy-start(s32[16,8]{0,1:T(8,128)} %param.12) | copy-start | bytes 1540
  39.2 36.9 %collective-permute-start.1 = (bf16[192,2048]{1,0:T(8,128)(2,1)}, bf16[192,2048]{1,0:T(8,128)(2,1)}, u32[]{:S(2)}, u32[]{:S(2)}) collective-permute-start(bf16[192,2048]{1,0:T(8,128)(2,1)} %pad_maximum_fusion.2.own_ref), channel_id=1, source_target_pairs={{0,28},{4,0},{8,4},{12,8},{16,12},{20,16},{24,20},{28,24},{1,29},{... | collective-permute-start | bytes 2359304 | tf_op jit(solution)/shard_map/ppermute | solution.py:279
  43.5 32.6 %collective-permute-start = (bf16[192,2048]{1,0:T(8,128)(2,1)}, bf16[192,2048]{1,0:T(8,128)(2,1)}, u32[]{:S(2)}, u32[]{:S(2)}) collective-permute-start(bf16[192,2048]{1,0:T(8,128)(2,1)} %pad_maximum_fusion.2.own_ref), channel_id=1, source_target_pairs={{0,4},{4,8},{8,12},{12,16},{16,20},{20,24},{24,28},{28,0},{1,5},{5... | collective-permute-start | bytes 2359304 | tf_op jit(solution)/shard_map/ppermute | solution.py:279
  44.6 31.5 %copy-start.1 = (s32[16]{0:T(128)S(1)}, s32[16]{0:T(128)}, u32[]{:S(2)}) copy-start(s32[16]{0:T(128)} %counts_ref.1) | copy-start | bytes 196
  44.6 11.0 %all-to-all-start = ((bf16[4,96,512]{2,1,0:T(8,128)(2,1)}), bf16[4,96,512]{2,1,0:T(8,128)(2,1)S(1)}, u32[]{:S(2)}, u32[]{:S(2)}) async-start(bf16[4,96,512]{2,1,0:T(8,128)(2,1)} %bitcast.71), calls=%async_computation | async-start | bytes 786432 | tf_op jit(solution)/shard_map/all_to_all | solution.py:302
  48.2 166.7 %reduce-scatter.2.cloned.1.call-start = ((), (), s32[]{:S(2)}) async-start(), calls=%async_computation.4 | async-start | bytes 1966080 | tf_op jit(solution)/shard_map/reduce_scatter | solution.py:342
  76.1 51.7 %copy-start.11 = (f32[2,3,2048]{2,1,0:T(4,128)S(1)}, f32[2,3,2048]{2,1,0:T(4,128)}, u32[]{:S(2)}) copy-start(f32[2,3,2048]{2,1,0:T(4,128)} %copy-done.10) | copy-start | bytes 147460
  123.2 37.2 %collective-permute-start.2 = (bf16[192,2048]{1,0:T(8,128)(2,1)}, bf16[192,2048]{1,0:T(8,128)(2,1)S(1)}, u32[]{:S(2)}, u32[]{:S(2)}) collective-permute-start(bf16[192,2048]{1,0:T(8,128)(2,1)} %get-tuple-element.16), channel_id=1, source_target_pairs={{0,28},{4,0},{8,4},{12,8},{16,12},{20,16},{24,20},{28,24},{1,29},{... | collective-permute-start | bytes 2359304 | tf_op jit(solution)/shard_map/ppermute | solution.py:279
  127.7 32.9 %collective-permute-start.3 = (bf16[192,2048]{1,0:T(8,128)(2,1)}, bf16[192,2048]{1,0:T(8,128)(2,1)S(1)}, u32[]{:S(2)}, u32[]{:S(2)}) collective-permute-start(bf16[192,2048]{1,0:T(8,128)(2,1)} %get-tuple-element.17), channel_id=1, source_target_pairs={{0,4},{4,8},{8,12},{12,16},{16,20},{20,24},{24,28},{28,0},{1,5},{5... | collective-permute-start | bytes 2359304 | tf_op jit(solution)/shard_map/ppermute | solution.py:279
  162.5 3.8 %copy-start.12 = (bf16[96,2048]{1,0:T(8,128)(2,1)}, bf16[96,2048]{1,0:T(8,128)(2,1)S(1)}, u32[]{:S(2)}) copy-start(bf16[96,2048]{1,0:T(8,128)(2,1)S(1)} %slice.45) | copy-start | bytes 1179652
  164.1 1.7 copy-start.3
  166.3 0.9 copy-start.9
  169.6 4.4 %copy-start.14 = (f32[384]{0:T(512)S(1)}, f32[384]{0:T(512)}, u32[]{:S(2)}) copy-start(f32[384]{0:T(512)} %param.8) | copy-start | bytes 4612
  169.6 12.2 %copy-start.4 = (bf16[512,384]{1,0:T(8,128)(2,1)S(1)}, bf16[512,384]{1,0:T(8,128)(2,1)}, u32[]{:S(2)}) copy-start(bf16[512,384]{1,0:T(8,128)(2,1)} %param.7) | copy-start | bytes 1179652
  169.6 12.2 %copy-start.8 = (bf16[384,384]{1,0:T(8,128)(2,1)S(1)}, bf16[384,384]{1,0:T(8,128)(2,1)}, u32[]{:S(2)}) copy-start(bf16[384,384]{1,0:T(8,128)(2,1)} %param.10) | copy-start | bytes 884740
  170.4 12.6 %copy-start.13 = (bf16[96,2048]{1,0:T(8,128)(2,1)S(1)}, bf16[96,2048]{1,0:T(8,128)(2,1)}, u32[]{:S(2)}) copy-start(bf16[96,2048]{1,0:T(8,128)(2,1)} %copy-done.12) | copy-start | bytes 1179652
  170.4 11.0 %all-to-all-start.1 = ((bf16[96,4,512]{2,0,1:T(8,128)(2,1)}), bf16[96,4,512]{2,0,1:T(8,128)(2,1)S(1)}, u32[]{:S(2)}, u32[]{:S(2)}) async-start(bf16[96,4,512]{2,0,1:T(8,128)(2,1)} %bitcast.55), calls=%async_computation.1 | async-start | bytes 786432 | tf_op jit(solution)/shard_map/all_to_all | solution.py:325
  181.4 1.6 copy-start.6
  183.0 33.1 %copy-start.15 = (f32[512]{0:T(512)S(1)}, f32[512]{0:T(512)}, u32[]{:S(2)}) copy-start(f32[512]{0:T(512)} %get-tuple-element.21) | copy-start | bytes 6148
Sparse Core Ops, SparseCore 0:
  11.1 22.3 all-gather.1
  169.7 30.1 reduce-scatter.1

commit v2 on v1

v2 whole, which is shorter than its diff:
```python
import functools
import math

import jax
import jax.numpy as jnp
from jax import lax
from jax.experimental import pallas as pl
from jax.experimental.pallas import tpu as pltpu
from jax.sharding import PartitionSpec as P

HEADS = 12
BLK = 128
REACH = 16
MESH = pl.DeviceIdType.MESH
F32, BF16 = jnp.float32, jnp.bfloat16

SCORE_SCALE = 10.0
LOG2E = 1.0 / math.log(2.0)
norm_eps = 1e-06


def dot(a, b):
    return jnp.dot(a, b, preferred_element_type=F32)


def attention_kernel(
    n_heads, hd, n_slots, lookup_ref, counts_ref, q_ref, do_ref, kv_ref,
    att_ref, dq_ref, g_ref,
    kv_t, k_n, v_n, dk_acc, dv_acc, e_s, ds_s,
):
    cols = n_heads * hd
    wide = n_heads * BLK
    ext = kv_ref.shape[1] // BLK

    @pl.loop(0, ext)
    def _(i):
        both = kv_ref[:, pl.ds(pl.multiple_of(i * BLK, BLK), BLK)]
        kv_t[i] = both
        k_n[i] = both[:cols].T
        v_n[i] = both[cols:].T
        zero = jnp.zeros((BLK, cols), F32)
        dk_acc[i] = zero
        dv_acc[i] = zero

    def diagonal(parts):
        rows = []
        for h in range(n_heads):
            zero = jnp.zeros((hd, BLK), BF16)
            rows.append(
                jnp.concatenate([parts[h] if g == h else zero for g in range(n_heads)], axis=1)
            )
        return jnp.concatenate(rows, axis=0)

    def of_head(value, h):
        return value[h * hd : (h + 1) * hd, h * BLK : (h + 1) * BLK]

    @pl.loop(0, q_ref.shape[1] // BLK)
    def _(b):
        at = pl.ds(pl.multiple_of(b * BLK, BLK), BLK)
        q_t = q_ref[:, at]
        do_t = do_ref[:, at]
        slots = [lookup_ref[b, j] for j in range(n_slots)]
        count = counts_ref[b]
        q_diag = diagonal([q_t[h * hd : (h + 1) * hd] for h in range(n_heads)])
        total = jnp.zeros((1, wide), F32)
        for j in range(n_slots):
            raised = jnp.exp2(dot(k_n[slots[j]], q_diag))
            raised = raised * jnp.where(j < count, 1.0, 0.0)
            total = total + jnp.sum(raised, axis=0, keepdims=True)
            e_s[j * BLK : (j + 1) * BLK, :] = raised.astype(BF16)
        values_t = jnp.concatenate([kv_t[s][cols:] for s in slots], axis=1)
        keys_t = jnp.concatenate([kv_t[s][:cols] for s in slots], axis=1)
        out = dot(values_t, e_s[...])
        share = 1.0 / total
        att, scaled, inner = [], [], []
        for h in range(n_heads):
            share_h = share[:, h * BLK : (h + 1) * BLK]
            att_h = of_head(out, h) * share_h
            do_h = do_t[h * hd : (h + 1) * hd].astype(F32) * share_h
            att.append(att_h)
            scaled.append(do_h.astype(BF16))
            inner.append(jnp.sum(att_h * do_h, axis=0, keepdims=True))
        att_ref[:, at] = jnp.concatenate(att, axis=0).astype(BF16)
        inner = jnp.concatenate(inner, axis=1)
        do_diag = diagonal(scaled)
        q_rows = q_diag.T
        do_rows = do_diag.T
        for j in range(n_slots):
            rows = slice(j * BLK, (j + 1) * BLK)
            e = e_s[rows, :]
            d = e.astype(F32) * (dot(v_n[slots[j]], do_diag) - inner)
            d = d.astype(BF16)
            ds_s[rows, :] = d
            dk_acc[slots[j]] += dot(d, q_rows)
            dv_acc[slots[j]] += dot(e, do_rows)
        dq = dot(keys_t, ds_s[...])
        dq = jnp.concatenate([of_head(dq, h) for h in range(n_heads)], axis=0)
        dq_ref[:, at] = (dq * SCORE_SCALE).astype(dq_ref.dtype)

    @pl.loop(0, ext)
    def _(i):
        at = pl.ds(pl.multiple_of(i * BLK, BLK), BLK)
        g_ref[:cols, at] = (dk_acc[i] * math.log(2.0)).T.astype(g_ref.dtype)
        g_ref[cols:, at] = dv_acc[i].T.astype(g_ref.dtype)


def attention(lookup, counts, q_t, do_t, kv_ext, hd):
    cols, rows = q_t.shape
    n_heads = cols // hd
    n_slots = lookup.shape[1]
    ext = kv_ext.shape[1] // BLK
    smem = pl.BlockSpec(memory_space=pltpu.SMEM)
    vmem = pl.BlockSpec(memory_space=pltpu.VMEM)
    shape = jax.ShapeDtypeStruct
    return pl.pallas_call(
        functools.partial(attention_kernel, n_heads, hd, n_slots),
        out_shape=(
            shape((cols, rows), BF16),
            shape((cols, rows), BF16),
            shape(kv_ext.shape, BF16),
        ),
        in_specs=[smem, smem] + [vmem] * 3,
        out_specs=(vmem,) * 3,
        scratch_shapes=[
            pltpu.VMEM((ext, 2 * cols, BLK), BF16),
            pltpu.VMEM((ext, BLK, cols), BF16),
            pltpu.VMEM((ext, BLK, cols), BF16),
            pltpu.VMEM((ext, BLK, cols), F32),
            pltpu.VMEM((ext, BLK, cols), F32),
            pltpu.VMEM((n_slots * BLK, n_heads * BLK), BF16),
            pltpu.VMEM((n_slots * BLK, n_heads * BLK), BF16),
        ],
        compiler_params=pltpu.CompilerParams(vmem_limit_bytes=52 * 1024 * 1024),
    )(lookup, counts, q_t, do_t, kv_ext)


def sender(src, dst, send_sem, recv_sem, target):
    copy = pltpu.make_async_remote_copy(
        src_ref=src, dst_ref=dst, send_sem=send_sem, recv_sem=recv_sem,
        device_id=target, device_id_type=MESH,
    )
    copy.start()
    return copy


def gather_kernel(
    n_slab, n_head, normed_ref, d_att_ref, ext_ref, d_heads_ref,
    h_send, h_recv, x_send, x_recv, c_send, c_recv, f_send, f_recv, a_send, a_recv,
):
    slab, head = lax.axis_index("slab"), lax.axis_index("head")
    up, down = lax.rem(slab + 1, n_slab), lax.rem(slab + n_slab - 1, n_slab)
    core = (head // 2) * 2 + 1 - lax.rem(head, 2)
    across = lax.rem(head + 2, n_head)
    rows = normed_ref.shape[0]
    cols = d_heads_ref.shape[0]

    barrier = pltpu.get_barrier_semaphore()
    for s in (up, down):
        pl.semaphore_signal(barrier, inc=1, device_id=(s, head), device_id_type=MESH)
    for k in range(1, n_head):
        pl.semaphore_signal(
            barrier, inc=1, device_id=(slab, lax.rem(head + k, n_head)), device_id_type=MESH
        )
    pl.semaphore_wait(barrier, n_head + 1)

    def at(t, h):
        return ext_ref.at[t, h]

    def spread(t, src):
        return (
            sender(src, at(t, head), x_send.at[t], x_recv.at[t], (slab, across)),
            sender(src, at(t, head), c_send.at[t], c_recv.at[t], (slab, core)),
        )

    def forward(t):
        return sender(
            at(t, across), at(t, across), f_send.at[t], f_recv.at[t], (slab, core)
        )

    own = spread(1, normed_ref)
    to_up = sender(normed_ref, at(0, head), h_send.at[0], h_recv.at[0], (up, head))
    to_down = sender(normed_ref, at(2, head), h_send.at[1], h_recv.at[1], (down, head))
    mine = pl.ds(pl.multiple_of(head * rows, 128), rows)
    sent = []
    for k in range(1, n_head):
        h = lax.rem(head + k, n_head)
        sent.append(
            sender(
                d_att_ref.at[pl.ds(pl.multiple_of(h * cols, 16), cols)],
                d_heads_ref.at[:, mine],
                a_send.at[k], a_recv.at[k], (slab, h),
            )
        )
    d_heads_ref[:, mine] = d_att_ref[pl.ds(pl.multiple_of(head * cols, 16), cols), :]
    ext_ref[1, head] = normed_ref[...]

    own[0].wait_recv()
    own_f = forward(1)
    to_up.wait_recv()
    low = spread(0, at(0, head))
    to_down.wait_recv()
    high = spread(2, at(2, head))
    low[0].wait_recv()
    low_f = forward(0)
    high[0].wait_recv()
    high_f = forward(2)
    for copy in (to_up, to_down, own[0], low[0], high[0]):
        copy.wait_send()
    for copy in (own[1], low[1], high[1], own_f, low_f, high_f, *sent):
        copy.wait()


def gather_slabs(normed, d_attended):
    n_slab, n_head = lax.axis_size("slab"), lax.axis_size("head")
    rows, width = normed.shape
    cols = width // n_head
    vmem = pl.BlockSpec(memory_space=pltpu.VMEM)
    shape = jax.ShapeDtypeStruct
    dma = pltpu.SemaphoreType.DMA
    return pl.pallas_call(
        functools.partial(gather_kernel, n_slab, n_head),
        out_shape=(
            shape((3, n_head, rows, width), BF16),
            shape((cols, n_head * rows), BF16),
        ),
        in_specs=[vmem] * 2,
        out_specs=(vmem,) * 2,
        scratch_shapes=[dma((2,))] * 2 + [dma((3,))] * 6 + [dma((n_head,))] * 2,
        compiler_params=pltpu.CompilerParams(
            collective_id=1, has_side_effects=True, vmem_limit_bytes=32 * 1024 * 1024
        ),
    )(normed, d_attended)


def sums_kernel(
    n_slab, n_head, att_ref, cot_ref, low_ref, own_ref, high_ref, qkv_ref, w_ref, gain_ref,
    attended_ref, dn_ref, d_qkv_ref, d_out_ref, d_gain_ref,
    pair_in, pair_out, x_in, rim_out, rim_in,
    out_part, heads_in, full, slabs_in, chunk, done_out, gain_part, gains_in, outs_in,
    p_send, p_recv, x_send, x_recv, r_send, r_recv, t_send, t_recv,
    send_a, recv_a, send_b, recv_b, send_c, recv_c, send_d, recv_d, send_e, recv_e,
):
    slab, head = lax.axis_index("slab"), lax.axis_index("head")
    up, down = lax.rem(slab + 1, n_slab), lax.rem(slab + n_slab - 1, n_slab)
    core = (head // 2) * 2 + 1 - lax.rem(head, 2)
    across = lax.rem(head + 2, n_head)
    corner = lax.rem(core + 2, n_head)
    rows_q = qkv_ref.shape[0]
    rows_o = att_ref.shape[0]
    step = chunk.shape[0]
    rows = dn_ref.shape[0]
    parts = (low_ref, own_ref, high_ref)

    def other_heads():
        return [(k, lax.rem(head + k, n_head)) for k in range(1, n_head)]

    def other_slabs():
        return [(k, lax.rem(slab + k, n_slab)) for k in range(1, n_slab)]

    def of(h):
        return pl.ds(pl.multiple_of(h * rows, 128), rows)

    def out_rows(h):
        return pl.ds(pl.multiple_of(h * rows_o, 16), rows_o)

    barrier = pltpu.get_barrier_semaphore()
    for _, h in other_heads():
        pl.semaphore_signal(barrier, inc=1, device_id=(slab, h), device_id_type=MESH)
    for _, s in other_slabs():
        pl.semaphore_signal(barrier, inc=1, device_id=(s, head), device_id_type=MESH)
    pl.semaphore_wait(barrier, n_head + n_slab - 2)

    def send_pair(t):
        return [
            sender(
                parts[t].at[of(h)], pair_in.at[t, i], p_send.at[t, i], p_recv.at[t, i],
                (slab, core),
            )
            for i, h in enumerate((corner, core))
        ]

    def pair_sum(t, copies):
        copies[0].wait()
        pair_out[t] = (
            parts[t][of(across), :].astype(F32) + pair_in[t, 0].astype(F32)
        ).astype(BF16)
        return sender(pair_out.at[t], x_in.at[t], x_send.at[t], x_recv.at[t], (slab, across))

    def whole_sum(t):
        return (
            parts[t][of(head), :].astype(F32)
            + pair_in[t, 1].astype(F32)
            + x_in[t].astype(F32)
        )

    sent = []
    for k, h in other_heads():
        sent.append(
            sender(
                att_ref.at[:, of(h)], attended_ref.at[out_rows(head)],
                t_send.at[k], t_recv.at[k], (slab, h),
            )
        )
    pairs = {t: send_pair(t) for t in (0, 2, 1)}
    attended_ref[out_rows(head), :] = att_ref[:, of(head)]
    x_low = pair_sum(0, pairs[0])
    x_high = pair_sum(2, pairs[2])

    for copy in sent:
        copy.wait()
    out_part[...] = dot(attended_ref[...], cot_ref[...]).astype(BF16)
    sent = []
    for k, h in other_heads():
        sent.append(
            sender(
                out_part.at[out_rows(h)], heads_in.at[k], send_a.at[k], recv_a.at[k], (slab, h)
            )
        )
    full[:rows_q, :] = qkv_ref[...]
    if full.shape[0] > rows_q + rows_o:
        full[rows_q + rows_o :, :] = jnp.zeros(
            (full.shape[0] - rows_q - rows_o, full.shape[1]), BF16
        )
    x_own = pair_sum(1, pairs[1])
    total = out_part[out_rows(head), :].astype(F32)
    for k in range(1, n_head):
        sent[k - 1].wait()
        total += heads_in[k].astype(F32)
    full[rows_q : rows_q + rows_o, :] = total.astype(BF16)
    sent = []
    for k, s in other_slabs():
        part = pl.ds(pl.multiple_of(s * step, 16), step)
        sent.append(sender(full.at[part], slabs_in.at[k], send_b.at[k], recv_b.at[k], (s, head)))

    pairs[0][1].wait()
    x_low.wait()
    rim_out[0] = whole_sum(0).astype(BF16)
    to_down = sender(rim_out.at[0], rim_in.at[0], r_send.at[0], r_recv.at[0], (down, head))
    pairs[2][1].wait()
    x_high.wait()
    rim_out[1] = whole_sum(2).astype(BF16)
    to_up = sender(rim_out.at[1], rim_in.at[1], r_send.at[1], r_recv.at[1], (up, head))

    mine = pl.ds(pl.multiple_of(slab * step, 16), step)
    total = full[mine, :].astype(F32)
    for k in range(1, n_slab):
        sent[k - 1].wait()
        total += slabs_in[k].astype(F32)
    chunk[...] = total.astype(BF16)
    sent = []
    for k, s in other_slabs():
        sent.append(sender(chunk, done_out.at[mine], send_c.at[k], recv_c.at[k], (s, head)))
    done_out[mine, :] = chunk[...]
    pairs[1][1].wait()
    x_own.wait()
    dn_ref[...] = whole_sum(1)
    for copy in sent:
        copy.wait()

    own = done_out.at[pl.ds(rows_q, rows_o)]
    sent = []
    for k, h in other_heads():
        sent.append(sender(own, outs_in.at[k], send_d.at[k], recv_d.at[k], (slab, h)))
    summed = done_out[:rows_q, :].astype(F32)
    part = jnp.sum(summed * w_ref[...].astype(F32), axis=0, keepdims=True) / gain_ref[...]
    gain_part[...] = jnp.broadcast_to(part, gain_part.shape)
    for k, h in other_heads():
        sent.append(sender(gain_part, gains_in.at[k], send_e.at[k], recv_e.at[k], (slab, h)))
    d_qkv_ref[...] = summed
    d_out_ref[out_rows(head), :] = done_out[rows_q : rows_q + rows_o, :].astype(F32)
    to_down.wait()
    to_up.wait()
    dn_ref[...] += rim_in[0].astype(F32) + rim_in[1].astype(F32)
    for copy in sent:
        copy.wait()
    gains_in[0] = gain_part[...]
    total = jnp.zeros(gain_part.shape, F32)
    for h in range(n_head):
        total += gains_in[lax.rem(head + n_head - h, n_head)]
    for k in range(1, n_head):
        source = lax.rem(head + n_head - k, n_head)
        d_out_ref[out_rows(source), :] = outs_in[k].astype(F32)
    d_gain_ref[...] = total


def grad_sums(att_t, cotangent, low, own, high, qkv_part, w_t, gain):
    n_slab, n_head = lax.axis_size("slab"), lax.axis_size("head")
    rows_q, width = qkv_part.shape
    rows_o = att_t.shape[0]
    rows = cotangent.shape[0]
    step = -(-(rows_q + rows_o) // (16 * n_slab)) * 16
    vmem = pl.BlockSpec(memory_space=pltpu.VMEM)
    shape = jax.ShapeDtypeStruct
    dma = pltpu.SemaphoreType.DMA
    return pl.pallas_call(
        functools.partial(sums_kernel, n_slab, n_head),
        out_shape=(
            shape((width, rows), BF16),
            shape((rows, width), F32),
            shape((rows_q, width), F32),
            shape((width, width), F32),
            shape((8, width), F32),
        ),
        in_specs=[vmem] * 8,
        out_specs=(vmem,) * 5,
        scratch_shapes=[
            pltpu.VMEM((3, 2, rows, width), BF16),
            pltpu.VMEM((3, rows, width), BF16),
            pltpu.VMEM((3, rows, width), BF16),
            pltpu.VMEM((2, rows, width), BF16),
            pltpu.VMEM((2, rows, width), BF16),
            pltpu.VMEM((width, width), BF16),
            pltpu.VMEM((n_head, rows_o, width), BF16),
            pltpu.VMEM((n_slab * step, width), BF16),
            pltpu.VMEM((n_slab, step, width), BF16),
            pltpu.VMEM((step, width), BF16),
            pltpu.VMEM((n_slab * step, width), BF16),
            pltpu.VMEM((8, width), F32),
            pltpu.VMEM((n_head, 8, width), F32),
            pltpu.VMEM((n_head, rows_o, width), BF16),
        ]
        + [dma((3, 2))] * 2 + [dma((3,))] * 2 + [dma((2,))] * 2 + [dma((n_head,))] * 4
        + [dma((n_slab,))] * 4 + [dma((n_head,))] * 4,
        compiler_params=pltpu.CompilerParams(
            collective_id=0, has_side_effects=True, vmem_limit_bytes=48 * 1024 * 1024
        ),
    )(att_t, cotangent, low, own, high, qkv_part, w_t, gain)


def over_rows(a, b):
    return lax.dot_general(a, b, (((0,), (0,)), ((), ())), preferred_element_type=F32)


def over_width(a, b):
    return lax.dot_general(a, b, (((1,), (1,)), ((), ())), preferred_element_type=F32)


def local(tokens, norm_gain, w_qkv, w_out, cotangent, neighbours, counts):
    width = tokens.shape[1]
    hd = width // HEADS
    n_head, n_slab = lax.axis_size("head"), lax.axis_size("slab")
    cols = width // n_head
    here = HEADS // n_head
    head_index, slab_index = lax.axis_index("head"), lax.axis_index("slab")
    slab_blocks = neighbours.shape[0]
    slab_rows = slab_blocks * BLK
    tok = tokens.astype(F32)
    inverse = lax.rsqrt(jnp.mean(tok * tok, -1, keepdims=True) + norm_eps)
    normed = (tok * inverse * norm_gain).astype(BF16)
    w_here = lax.dynamic_slice_in_dim(w_qkv, head_index * cols, cols, 2)
    w_t = w_here.transpose(0, 2, 1).reshape(3 * cols, width)
    d_attended = over_width(w_out, cotangent).astype(BF16)
    gathered, d_heads = gather_slabs(normed, d_attended)
    gathered = gathered.reshape(3 * slab_rows, width)
    own_rows = gathered[slab_rows : 2 * slab_rows]

    floor = 0.7 * math.sqrt(hd)

    def unit_of(projected):
        by_head = projected.reshape(here, hd, -1)
        length = jnp.sqrt(jnp.sum(by_head * by_head, 1, keepdims=True))
        divisor = jnp.maximum(length, floor)
        return by_head / divisor, divisor, length > floor

    def unit_back(parts, grad):
        unit, divisor, active = parts
        along = grad.astype(F32).reshape(unit.shape)
        inner = jnp.sum(unit * along, 1, keepdims=True)
        result = (along - jnp.where(active, unit * inner, 0.0)) / divisor
        return result.reshape(grad.shape).astype(BF16)

    q_parts = unit_of(over_width(w_t[:cols], own_rows))
    kv = over_width(w_t[cols:], gathered)
    k_parts = unit_of(kv[:cols])
    q_t = (q_parts[0] * (SCORE_SCALE * LOG2E)).reshape(cols, slab_rows).astype(BF16)
    kv_ext = jnp.concatenate(
        [k_parts[0].reshape(cols, 3 * slab_rows).astype(BF16), kv[cols:].astype(BF16)], 0
    )
    lookup = (neighbours - slab_index * slab_blocks + REACH) % (slab_blocks * n_slab)
    att_t, dq_t, g_kv = attention(lookup, counts, q_t, d_heads, kv_ext, hd)

    d_q = unit_back(q_parts, dq_t)
    d_kv = jnp.concatenate([unit_back(k_parts, g_kv[:cols]), g_kv[cols:]], 0)
    low, high = d_kv[:, :slab_rows], d_kv[:, 2 * slab_rows :]
    own = jnp.concatenate([d_q, d_kv[:, slab_rows : 2 * slab_rows]], 0)
    qkv_part = jnp.concatenate([dot(d_q, own_rows), dot(d_kv, gathered)], 0).astype(BF16)
    attended, d_normed, d_w, d_w_out, d_gain = grad_sums(
        att_t,
        cotangent,
        over_rows(low, w_t[cols:]).astype(BF16),
        over_rows(own, w_t).astype(BF16),
        over_rows(high, w_t[cols:]).astype(BF16),
        qkv_part,
        w_t,
        norm_gain.reshape(1, width),
    )
    output = (tok + over_rows(attended, w_out)).astype(BF16)
    d_w_qkv = d_w.reshape(3, cols, width).transpose(0, 2, 1)
    scaled = d_normed * norm_gain
    d_tokens = (
        cotangent.astype(F32)
        + inverse * scaled
        - tok * inverse**3 * jnp.mean(scaled * tok, -1, keepdims=True)
    )
    return (output, d_tokens.astype(BF16), d_w_qkv, d_w_out, d_gain[0])


def solution(mesh):
    placed = (
        P(("slab", "head"), None),
        P(),
        P(),
        P(),
        P(("slab", "head"), None),
        P("slab", None),
        P("slab"),
    )
    return jax.shard_map(
        local,
        mesh=mesh,
        in_specs=placed,
        out_specs=(
            P(("slab", "head"), None),
            P(("slab", "head"), None),
            P(None, None, "head"),
            P(),
            P(),
        ),
        check_vma=False,
    )
```

time: 228 us -> 183 us (0.80)
  waiting for transfers between devices: 90 us -> 0 us
  Pallas kernels: 76.5 us -> 152 us
  starting transfers between devices: 16 us -> 0 us
  between operations: 14.4 us -> 0.96 us
    ppermute x4 -> x0, waiting for transfers between devices: 53.1 us -> none  [shifted(): lax.ppermute(value, 'slab', [(i, (i + steps) % size) for i in range(size)])]
    pallas_call x0 -> x1, Pallas kernels: none -> 39 us  [gather_slabs(): pl.pallas_call(functools.partial(gather_kernel, n_slab, n_head), out_shap...]
    pallas_call x1, Pallas kernels: 29.4 us -> 65.5 us  [grad_sums(): pl.pallas_call(functools.partial(sums_kernel, n_slab, n_head), out_shape=...]
    all_gather x1 -> x0, waiting for transfers between devices: 22.1 us -> none  [local(): gathered = lax.all_gather(normed, 'head', axis=0, tiled=True)]
    all_to_all x2 -> x0, waiting for transfers between devices: 14.6 us -> none  [the longest x1 7.39 us: local(): lax.all_to_all(attended_t, 'head', split_axis=1, concat_axis=0, tiled=True)]
    ppermute x4 -> x0, starting transfers between devices: 8.74 us -> none  [shifted(): lax.ppermute(value, 'slab', [(i, (i + steps) % size) for i in range(size)])]
    all_to_all x2 -> x0, starting transfers between devices: 7.18 us -> none  [the longest x1 3.59 us: local(): lax.all_to_all(d_attended, 'head', split_axis=0, concat_axis=1, tiled=True)]
    mul x1 -> x2, other arithmetic: 1.57 us -> 4.67 us  [unit_back(): result = (along - jnp.where(active, unit * inner, 0.0)) / divisor]
  transfers between devices with their start and end apart: 8 -> 0, of which waited for: 6 -> 0; matrix products, arithmetic and copies ran while one was open for 3% -> 0% of each run, Pallas kernels for 13% -> 0%
where the time goes in v2:
time: 183 us
  Pallas kernels  152 us (83%)
  other arithmetic  11.7 us (6%)
  matrix products  10.8 us (6%)
  local copies, waits for them, and re-layouts  8.09 us (4%)
    pallas_call x1, Pallas kernels, grad_sums(): pl.pallas_call(functools.partial(sums_kernel, n_slab, n_head), out_shape=...  65.5 us
    pallas_call x1, Pallas kernels, attention(): pl.pallas_call(functools.partial(attention_kernel, n_heads, hd, n_slots),...  47 us
    pallas_call x1, Pallas kernels, gather_slabs(): pl.pallas_call(functools.partial(gather_kernel, n_slab, n_head), out_shap...  39 us
    dot_general x4, matrix products, over_rows(): lax.dot_general(a, b, (((0,), (0,)), ((), ())), preferred_element_type=F32)  6.21 us
    unnamed x28, local copies, waits for them, and re-layouts  6.06 us
    mul x2, other arithmetic, unit_back(): result = (along - jnp.where(active, unit * inner, 0.0)) / divisor  4.67 us

profile of v2, /device:TPU:0, one launch (start us, length us, event | category | flops | bytes accessed | tf_op | source)
XLA Modules:
  0.0 183.1 jit_solution(5452577671359686506)
XLA Ops:
  0.6 0.0 copy-start
  0.6 0.0 copy-start.1
  0.7 0.0 copy-start.8
  0.7 0.8 broadcast_in_dim.41.gain_ref
  1.5 1.1 fusion.19
  2.6 0.8 copy.15
  3.4 0.0 copy-done
  3.4 0.2 constant_dynamic-slice_fusion
  3.6 0.2 copy.17
  3.8 1.2 fusion.21.normed_ref
  5.0 0.0 copy-done.1
  5.0 0.0 copy-done.8
  5.0 0.4 convolution_convert_fusion.3.d_att_ref
  5.4 39.0 %shard_map.110 = (bf16[3,4,512,384]{3,2,1,0:T(8,128)(2,1)S(1)}, bf16[96,2048]{1,0:T(8,128)(2,1)S(1)}) custom-call(bf16[512,384]{1,0:T(8,128)(2,1)S(1)} %fusion.21.normed_ref, bf16[384,512]{1,0:T(8,128)(2,1)S(1)} %convolution_convert_fusion.3.d_att_ref), custom_call_target="tpu_custom_call" | custom-call | tf_op jit(solution)/shard_map/pallas_call | solution.py:220
  44.5 0.2 slice.44
  44.6 0.6 multiply_reduce_fusion.2
  45.3 0.1 multiply_convert_fusion
  45.4 1.8 fusion.37
  47.2 0.0 copy-start.3
  47.2 0.1 slice.95
  47.4 0.2 slice.58
  47.5 0.0 copy-start.5
  47.6 1.6 copy-done.5
  49.2 0.3 multiply_reduce_fusion.1
  49.5 0.1 sqrt_compare_fusion
  49.6 0.1 sqrt_maximum_fusion
  49.6 0.4 copy-done.3
  50.1 0.2 fusion.18
  50.3 0.0 copy-start.2
  50.3 1.6 pad_maximum_fusion.2.kv_ref
  51.9 0.0 copy-done.2
  51.9 47.0 %shard_map.111 = (bf16[96,2048]{1,0:T(8,128)(2,1)S(1)}, bf16[96,2048]{1,0:T(8,128)(2,1)S(1)}, bf16[192,6144]{1,0:T(8,128)(2,1)}) custom-call(s32[16,8]{1,0:T(8,128)S(1)} %add_select_fusion.lookup_ref, s32[16]{0:T(128)S(1)} %copy-done.2, bf16[96,2048]{1,0:T(8,128)(2,1)S(1)} %bitcast.57, bf16[96,2048]{1,0:T(8,128)(2,1)S(1)} %get-tuple-element.16.do_ref, ...), custom_call_target="tpu_custom_call" | custom-call | tf_op jit(solution)/shard_map/pallas_call | solution.py:115
  98.9 0.0 copy-start.7
  98.9 0.3 fusion.11
  99.2 0.0 copy-start.6
  99.2 0.4 convolution_convert_fusion.4
  99.6 0.9 copy-done.7
  100.6 0.0 slice-start
  100.6 0.3 fusion.36
  100.9 0.5 copy-done.6
  101.4 0.0 slice-start.1
  101.4 4.4 %fusion.1 = f32[3,32,6144]{2,1,0:T(8,128)S(1)} fusion(f32[3,32,6144]{2,1,0:T(8,128)S(1)} %bitcast.69, f32[3,32,6144]{2,1,0:T(8,128)S(1)} %bitcast.65, f32[3,6144]{1,0:T(4,128)S(1)} %sqrt_maximum_fusion), kind=kOutput, calls=%fused_computation.1 | output fusion | flops 1198111 | bytes 7151616 | tf_op jit(solution)/shard_map/mul | solution.py:469
  105.7 0.0 slice-done
  105.8 0.0 slice-done.1
  105.8 0.6 fusion.7
  106.4 1.4 fusion.16
  107.9 0.1 fusion.28
  107.9 2.3 %convolution_convert_fusion.own_ref = bf16[2048,384]{1,0:T(8,128)(2,1)} fusion(bf16[288,384]{1,0:T(8,128)(2,1)S(1)} %bitcast.55, bf16[192,2048]{1,0:T(8,128)(2,1)S(1)} %fusion.28, bf16[96,2048]{1,0:T(8,128)(2,1)S(1)} %bitcast.71), kind=kOutput, calls=%fused_computation.11 | convolution fusion | flops 456130560 | bytes 2973696 | tf_op jit(solution)/shard_map/dot_general | solution.py:431
  110.3 0.8 convolution_convert_fusion.2.low_ref
  111.0 1.9 %convolution_convert_fusion.1.high_ref = bf16[2048,384]{1,0:T(8,128)(2,1)} fusion(bf16[192,384]{1,0:T(8,128)(2,1)S(1)} %bitcast.68, bf16[96,6144]{1,0:T(8,128)(2,1)S(1)} %fusion.7, bf16[96,6144]{1,0:T(8,128)(2,1)S(1)} %get-tuple-element.25), kind=kOutput, calls=%fused_computation.12 | convolution fusion | flops 304349184 | bytes 4079616 | tf_op jit(solution)/shard_map/dot_general | solution.py:431
  112.9 0.0 copy-start.4
  112.9 0.0 copy-start.9
  112.9 65.5 %shard_map.112 = (bf16[384,512]{1,0:T(8,128)(2,1)S(1)}, f32[512,384]{1,0:T(8,128)S(1)}, f32[288,384]{1,0:T(8,128)S(1)}, f32[384,384]{1,0:T(8,128)S(1)}, f32[8,384]{1,0:T(8,128)S(1)}) custom-call(bf16[96,2048]{1,0:T(8,128)(2,1)S(1)} %get-tuple-element.17.att_ref, bf16[512,384]{1,0:T(8,128)(2,1)S(1)} %copy-done.1, ...), custom_call_target="tpu_custom_call" | custom-call | tf_op jit(solution)/shard_map/pallas_call | solution.py:395
  178.4 0.0 copy-done.4
  178.5 1.2 fusion.12
  179.7 0.6 slice_reduce_fusion
  180.3 0.0 copy-done.9
  180.3 0.2 fusion.25
  180.5 1.1 fusion.24
  181.6 0.8 copy.20
  182.3 0.8 copy.21
  (9 shorter events, 0.1 us)
Async XLA Ops:
  0.6 2.8 %copy-start = (bf16[3,384,384]{2,1,0:T(8,128)(2,1)S(1)}, bf16[3,384,384]{2,1,0:T(8,128)(2,1)}, u32[]{:S(2)}) copy-start(bf16[3,384,384]{2,1,0:T(8,128)(2,1)} %param.9) | copy-start | bytes 2654212
  0.6 4.3 %copy-start.1 = (bf16[512,384]{1,0:T(8,128)(2,1)S(1)}, bf16[512,384]{1,0:T(8,128)(2,1)}, u32[]{:S(2)}) copy-start(bf16[512,384]{1,0:T(8,128)(2,1)} %cot_ref.1) | copy-start | bytes 1179652
  0.7 4.3 %copy-start.8 = (bf16[384,384]{1,0:T(8,128)(2,1)S(1)}, bf16[384,384]{1,0:T(8,128)(2,1)}, u32[]{:S(2)}) copy-start(bf16[384,384]{1,0:T(8,128)(2,1)} %param.10) | copy-start | bytes 884740
  47.2 2.8 %copy-start.3 = (f32[192,6144]{1,0:T(8,128)}, f32[192,6144]{1,0:T(8,128)S(1)}, u32[]{:S(2)}) copy-start(f32[192,6144]{1,0:T(8,128)S(1)} %fusion.37) | copy-start | bytes 14155780
  47.5 1.6 copy-start.5
  50.3 1.6 copy-start.2
  98.9 1.7 copy-start.7
  99.2 2.2 %copy-start.6 = (f32[96,6144]{1,0:T(8,128)S(1)}, f32[96,6144]{1,0:T(8,128)}, u32[]{:S(2)}) copy-start(f32[96,6144]{1,0:T(8,128)} %copy-done.5) | copy-start | bytes 7077892
  100.6 5.2 %slice-start = ((s8[4718592]{0:T(1024)(128)(4,1)}), s8[4194304]{0:T(1024)(128)(4,1)S(1)}, s32[]{:S(2)}) async-start(s8[4718592]{0:T(1024)(128)(4,1)} %bitcast.60), calls=%async_computation | async-start | bytes 8388608
  101.4 4.4 %slice-start.1 = ((s8[4718592]{0:T(1024)(128)(4,1)}), s8[524288]{0:T(1024)(128)(4,1)S(1)}, s32[]{:S(2)}) async-start(s8[4718592]{0:T(1024)(128)(4,1)} %bitcast.60), calls=%async_computation.1 | async-start | bytes 1048576
  112.9 65.5 %copy-start.4 = (bf16[512,384]{1,0:T(8,128)(2,1)S(1)}, bf16[512,384]{1,0:T(8,128)(2,1)}, u32[]{:S(2)}) copy-start(bf16[512,384]{1,0:T(8,128)(2,1)} %param.7) | copy-start | bytes 1179652
  112.9 67.3 %copy-start.9 = (f32[384]{0:T(512)S(1)}, f32[384]{0:T(512)}, u32[]{:S(2)}) copy-start(f32[384]{0:T(512)} %param.8) | copy-start | bytes 4612

commit v3 on v2

--- a/solution.py
+++ b/solution.py
@@ -163,24 +163,41 @@
         )
     pl.semaphore_wait(barrier, n_head + 1)
 
-    def at(t, h):
-        return ext_ref.at[t, h]
-
-    def spread(t, src):
-        return (
-            sender(src, at(t, head), x_send.at[t], x_recv.at[t], (slab, across)),
-            sender(src, at(t, head), c_send.at[t], c_recv.at[t], (slab, core)),
-        )
-
-    def forward(t):
+    n_chunks = h_send.shape[1]
+    size = rows // n_chunks
+
+    def at(t, h, c):
+        return ext_ref.at[t, h, pl.ds(c * size, size)]
+
+    def spread(t, c, src):
+        return [
+            sender(src, at(t, head, c), x_send.at[t, c], x_recv.at[t, c], (slab, across)),
+            sender(src, at(t, head, c), c_send.at[t, c], c_recv.at[t, c], (slab, core)),
+        ]
+
+    def forward(t, c):
         return sender(
-            at(t, across), at(t, across), f_send.at[t], f_recv.at[t], (slab, core)
-        )
-
-    own = spread(1, normed_ref)
-    to_up = sender(normed_ref, at(0, head), h_send.at[0], h_recv.at[0], (up, head))
-    to_down = sender(normed_ref, at(2, head), h_send.at[1], h_recv.at[1], (down, head))
+            at(t, across, c), at(t, across, c), f_send.at[t, c], f_recv.at[t, c], (slab, core)
+        )
+
+    own, low, high, to_up, to_down, ahead = [], [], [], [], [], []
+    for c in range(n_chunks):
+        src = normed_ref.at[pl.ds(c * size, size)]
+        to_up.append(sender(src, at(0, head, c), h_send.at[0, c], h_recv.at[0, c], (up, head)))
+        to_down.append(
+            sender(src, at(2, head, c), h_send.at[1, c], h_recv.at[1, c], (down, head))
+        )
+        own.append(spread(1, c, src))
     mine = pl.ds(pl.multiple_of(head * rows, 128), rows)
+    d_heads_ref[:, mine] = d_att_ref[pl.ds(pl.multiple_of(head * cols, 16), cols), :]
+    ext_ref[1, head] = normed_ref[...]
+    for c in range(n_chunks):
+        to_up[c].wait_recv()
+        low.append(spread(0, c, at(0, head, c)))
+        to_down[c].wait_recv()
+        high.append(spread(2, c, at(2, head, c)))
+        own[c][0].wait_recv()
+        ahead.append(forward(1, c))
     sent = []
     for k in range(1, n_head):
         h = lax.rem(head + k, n_head)
@@ -191,22 +208,17 @@
                 a_send.at[k], a_recv.at[k], (slab, h),
             )
         )
-    d_heads_ref[:, mine] = d_att_ref[pl.ds(pl.multiple_of(head * cols, 16), cols), :]
-    ext_ref[1, head] = normed_ref[...]
-
-    own[0].wait_recv()
-    own_f = forward(1)
-    to_up.wait_recv()
-    low = spread(0, at(0, head))
-    to_down.wait_recv()
-    high = spread(2, at(2, head))
-    low[0].wait_recv()
-    low_f = forward(0)
-    high[0].wait_recv()
-    high_f = forward(2)
-    for copy in (to_up, to_down, own[0], low[0], high[0]):
-        copy.wait_send()
-    for copy in (own[1], low[1], high[1], own_f, low_f, high_f, *sent):
+    for c in range(n_chunks):
+        low[c][0].wait_recv()
+        ahead.append(forward(0, c))
+        high[c][0].wait_recv()
+        ahead.append(forward(2, c))
+    for c in range(n_chunks):
+        for copy in (to_up[c], to_down[c], own[c][0], low[c][0], high[c][0]):
+            copy.wait_send()
+        for copy in (own[c][1], low[c][1], high[c][1]):
+            copy.wait()
+    for copy in (*ahead, *sent):
         copy.wait()
 
 
@@ -225,7 +237,7 @@
         ),
         in_specs=[vmem] * 2,
         out_specs=(vmem,) * 2,
-        scratch_shapes=[dma((2,))] * 2 + [dma((3,))] * 6 + [dma((n_head,))] * 2,
+        scratch_shapes=[dma((2, 4))] * 2 + [dma((3, 4))] * 6 + [dma((n_head,))] * 2,
         compiler_params=pltpu.CompilerParams(
             collective_id=1, has_side_effects=True, vmem_limit_bytes=32 * 1024 * 1024
         ),
@@ -270,27 +282,45 @@
         pl.semaphore_signal(barrier, inc=1, device_id=(s, head), device_id_type=MESH)
     pl.semaphore_wait(barrier, n_head + n_slab - 2)
 
-    def send_pair(t):
-        return [
-            sender(
-                parts[t].at[of(h)], pair_in.at[t, i], p_send.at[t, i], p_recv.at[t, i],
-                (slab, core),
-            )
-            for i, h in enumerate((corner, core))
-        ]
-
-    def pair_sum(t, copies):
-        copies[0].wait()
-        pair_out[t] = (
-            parts[t][of(across), :].astype(F32) + pair_in[t, 0].astype(F32)
+    n_chunks = x_send.shape[1]
+    size = rows // n_chunks
+
+    def span(c):
+        return pl.ds(c * size, size)
+
+    def of_chunk(h, c):
+        return pl.ds(pl.multiple_of(h * rows + c * size, 128), size)
+
+    def send_pair(t, c, i):
+        return sender(
+            parts[t].at[of_chunk((corner, core)[i], c)], pair_in.at[t, i, span(c)],
+            p_send.at[t, i, c], p_recv.at[t, i, c], (slab, core),
+        )
+
+    def pair_sum(t, c, copy):
+        copy.wait()
+        pair_out[t, span(c)] = (
+            parts[t][of_chunk(across, c), :].astype(F32) + pair_in[t, 0, span(c)].astype(F32)
         ).astype(BF16)
-        return sender(pair_out.at[t], x_in.at[t], x_send.at[t], x_recv.at[t], (slab, across))
-
-    def whole_sum(t):
+        return sender(
+            pair_out.at[t, span(c)], x_in.at[t, span(c)],
+            x_send.at[t, c], x_recv.at[t, c], (slab, across),
+        )
+
+    def whole_sum(t, c):
         return (
-            parts[t][of(head), :].astype(F32)
-            + pair_in[t, 1].astype(F32)
-            + x_in[t].astype(F32)
+            parts[t][of_chunk(head, c), :].astype(F32)
+            + pair_in[t, 1, span(c)].astype(F32)
+            + x_in[t, span(c)].astype(F32)
+        )
+
+    def rim(i, t, c, target):
+        pairs[t, c, 1].wait()
+        crossing[t, c].wait()
+        rim_out[i, span(c)] = whole_sum(t, c).astype(BF16)
+        return sender(
+            rim_out.at[i, span(c)], rim_in.at[i, span(c)],
+            r_send.at[i, c], r_recv.at[i, c], (target, head),
         )
 
     sent = []
@@ -301,10 +331,21 @@
                 t_send.at[k], t_recv.at[k], (slab, h),
             )
         )
-    pairs = {t: send_pair(t) for t in (0, 2, 1)}
+    pairs, crossing, rims = {}, {}, []
+    order = [(t, c) for c in range(n_chunks) for t in (0, 2)]
+    order += [(1, c) for c in range(n_chunks)]
+    for i in range(2):
+        for t, c in order:
+            pairs[t, c, i] = send_pair(t, c, i)
     attended_ref[out_rows(head), :] = att_ref[:, of(head)]
-    x_low = pair_sum(0, pairs[0])
-    x_high = pair_sum(2, pairs[2])
+    full[:rows_q, :] = qkv_ref[...]
+    if full.shape[0] > rows_q + rows_o:
+        full[rows_q + rows_o :, :] = jnp.zeros(
+            (full.shape[0] - rows_q - rows_o, full.shape[1]), BF16
+        )
+    half = len(order) // 3
+    for t, c in order[:half]:
+        crossing[t, c] = pair_sum(t, c, pairs[t, c, 0])
 
     for copy in sent:
         copy.wait()
@@ -316,12 +357,11 @@
                 out_part.at[out_rows(h)], heads_in.at[k], send_a.at[k], recv_a.at[k], (slab, h)
             )
         )
-    full[:rows_q, :] = qkv_ref[...]
-    if full.shape[0] > rows_q + rows_o:
-        full[rows_q + rows_o :, :] = jnp.zeros(
-            (full.shape[0] - rows_q - rows_o, full.shape[1]), BF16
-        )
-    x_own = pair_sum(1, pairs[1])
+    for t, c in order[half:]:
+        crossing[t, c] = pair_sum(t, c, pairs[t, c, 0])
+    for t, c in order[:half]:
+        rims.append(rim(t // 2, t, c, (down, None, up)[t]))
+
     total = out_part[out_rows(head), :].astype(F32)
     for k in range(1, n_head):
         sent[k - 1].wait()
@@ -331,15 +371,8 @@
     for k, s in other_slabs():
         part = pl.ds(pl.multiple_of(s * step, 16), step)
         sent.append(sender(full.at[part], slabs_in.at[k], send_b.at[k], recv_b.at[k], (s, head)))
-
-    pairs[0][1].wait()
-    x_low.wait()
-    rim_out[0] = whole_sum(0).astype(BF16)
-    to_down = sender(rim_out.at[0], rim_in.at[0], r_send.at[0], r_recv.at[0], (down, head))
-    pairs[2][1].wait()
-    x_high.wait()
-    rim_out[1] = whole_sum(2).astype(BF16)
-    to_up = sender(rim_out.at[1], rim_in.at[1], r_send.at[1], r_recv.at[1], (up, head))
+    for t, c in order[half : 2 * half]:
+        rims.append(rim(t // 2, t, c, (down, None, up)[t]))
 
     mine = pl.ds(pl.multiple_of(slab * step, 16), step)
     total = full[mine, :].astype(F32)
@@ -351,9 +384,10 @@
     for k, s in other_slabs():
         sent.append(sender(chunk, done_out.at[mine], send_c.at[k], recv_c.at[k], (s, head)))
     done_out[mine, :] = chunk[...]
-    pairs[1][1].wait()
-    x_own.wait()
-    dn_ref[...] = whole_sum(1)
+    for t, c in order[2 * half :]:
+        pairs[t, c, 1].wait()
+        crossing[t, c].wait()
+        dn_ref[span(c), :] = whole_sum(t, c)
     for copy in sent:
         copy.wait()
 
@@ -368,8 +402,8 @@
         sent.append(sender(gain_part, gains_in.at[k], send_e.at[k], recv_e.at[k], (slab, h)))
     d_qkv_ref[...] = summed
     d_out_ref[out_rows(head), :] = done_out[rows_q : rows_q + rows_o, :].astype(F32)
-    to_down.wait()
-    to_up.wait()
+    for copy in rims:
+        copy.wait()
     dn_ref[...] += rim_in[0].astype(F32) + rim_in[1].astype(F32)
     for copy in sent:
         copy.wait()
@@ -419,7 +453,7 @@
             pltpu.VMEM((n_head, 8, width), F32),
             pltpu.VMEM((n_head, rows_o, width), BF16),
         ]
-        + [dma((3, 2))] * 2 + [dma((3,))] * 2 + [dma((2,))] * 2 + [dma((n_head,))] * 4
+        + [dma((3, 2, 4))] * 2 + [dma((3, 4))] * 2 + [dma((2, 4))] * 2 + [dma((n_head,))] * 4
         + [dma((n_slab,))] * 4 + [dma((n_head,))] * 4,
         compiler_params=pltpu.CompilerParams(
             collective_id=0, has_side_effects=True, vmem_limit_bytes=48 * 1024 * 1024

time: 183 us -> 164 us (0.90)
  Pallas kernels: 152 us -> 132 us
    pallas_call x1, Pallas kernels: 65.5 us -> 48.1 us  [grad_sums(): pl.pallas_call(functools.partial(sums_kernel, n_slab, n_head), out_shape=...]
where the time goes in v3:
time: 164 us
  Pallas kernels  132 us (80%)
  other arithmetic  11.7 us (7%)
  matrix products  10.8 us (7%)
  local copies, waits for them, and re-layouts  8.09 us (5%)
    pallas_call x1, Pallas kernels, grad_sums(): pl.pallas_call(functools.partial(sums_kernel, n_slab, n_head), out_shape=...  48.1 us
    pallas_call x1, Pallas kernels, attention(): pl.pallas_call(functools.partial(attention_kernel, n_heads, hd, n_slots),...  47 us
    pallas_call x1, Pallas kernels, gather_slabs(): pl.pallas_call(functools.partial(gather_kernel, n_slab, n_head), out_shap...  37.2 us
    dot_general x4, matrix products, over_rows(): lax.dot_general(a, b, (((0,), (0,)), ((), ())), preferred_element_type=F32)  6.2 us
    unnamed x28, local copies, waits for them, and re-layouts  6.06 us
    mul x2, other arithmetic, unit_back(): result = (along - jnp.where(active, unit * inner, 0.0)) / divisor  4.67 us

profile of v3, /device:TPU:0, one launch (start us, length us, event | category | flops | bytes accessed | tf_op | source)
XLA Modules:
  0.0 163.9 jit_solution(2483870487802115293)
XLA Ops:
  0.6 0.0 copy-start
  0.6 0.0 copy-start.1
  0.7 0.0 copy-start.8
  0.7 0.8 broadcast_in_dim.41.gain_ref
  1.5 1.1 fusion.19
  2.6 0.8 copy.15
  3.4 0.0 copy-done
  3.4 0.2 constant_dynamic-slice_fusion
  3.6 0.2 copy.17
  3.8 1.2 fusion.21.normed_ref
  5.0 0.0 copy-done.1
  5.0 0.0 copy-done.8
  5.0 0.4 convolution_convert_fusion.3.d_att_ref
  5.4 37.2 %shard_map.110 = (bf16[3,4,512,384]{3,2,1,0:T(8,128)(2,1)S(1)}, bf16[96,2048]{1,0:T(8,128)(2,1)S(1)}) custom-call(bf16[512,384]{1,0:T(8,128)(2,1)S(1)} %fusion.21.normed_ref, bf16[384,512]{1,0:T(8,128)(2,1)S(1)} %convolution_convert_fusion.3.d_att_ref), custom_call_target="tpu_custom_call" | custom-call | tf_op jit(solution)/shard_map/pallas_call | solution.py:232
  42.6 0.2 slice.44
  42.8 0.6 multiply_reduce_fusion.2
  43.5 0.1 multiply_convert_fusion
  43.6 1.8 %fusion.37 = f32[192,6144]{1,0:T(8,128)S(1)} fusion(bf16[192,384]{1,0:T(8,128)(2,1)S(1)} %bitcast.66, bf16[6144,384]{1,0:T(8,128)(2,1)S(1)} %bitcast.51), kind=kOutput, calls=%fused_computation.78 | convolution fusion | flops 905969664 | bytes 9584640 | tf_op jit(solution)/shard_map/dot_general | solution.py:469
  45.4 0.0 copy-start.3
  45.4 0.1 slice.95
  45.6 0.2 slice.58
  45.7 0.0 copy-start.5
  45.7 1.6 copy-done.5
  47.4 0.3 multiply_reduce_fusion.1
  47.7 0.1 sqrt_compare_fusion
  47.8 0.1 sqrt_maximum_fusion
  47.8 0.4 copy-done.3
  48.3 0.2 fusion.18
  48.5 0.0 copy-start.2
  48.5 1.6 pad_maximum_fusion.2.kv_ref
  50.1 0.0 copy-done.2
  50.1 47.0 %shard_map.111 = (bf16[96,2048]{1,0:T(8,128)(2,1)S(1)}, bf16[96,2048]{1,0:T(8,128)(2,1)S(1)}, bf16[192,6144]{1,0:T(8,128)(2,1)}) custom-call(s32[16,8]{1,0:T(8,128)S(1)} %add_select_fusion.lookup_ref, s32[16]{0:T(128)S(1)} %copy-done.2, bf16[96,2048]{1,0:T(8,128)(2,1)S(1)} %bitcast.57, bf16[96,2048]{1,0:T(8,128)(2,1)S(1)} %get-tuple-element.16.do_ref, ...), custom_call_target="tpu_custom_call" | custom-call | tf_op jit(solution)/shard_map/pallas_call | solution.py:115
  97.1 0.0 copy-start.7
  97.1 0.3 fusion.11
  97.4 0.0 copy-start.6
  97.4 0.4 convolution_convert_fusion.4
  97.8 0.9 copy-done.7
  98.8 0.0 slice-start
  98.8 0.3 fusion.36
  99.1 0.5 copy-done.6
  99.5 0.0 slice-start.1
  99.5 4.4 %fusion.1 = f32[3,32,6144]{2,1,0:T(8,128)S(1)} fusion(f32[3,32,6144]{2,1,0:T(8,128)S(1)} %bitcast.69, f32[3,32,6144]{2,1,0:T(8,128)S(1)} %bitcast.65, f32[3,6144]{1,0:T(4,128)S(1)} %sqrt_maximum_fusion), kind=kOutput, calls=%fused_computation.1 | output fusion | flops 1198111 | bytes 7151616 | tf_op jit(solution)/shard_map/mul | solution.py:503
  103.9 0.0 slice-done
  103.9 0.0 slice-done.1
  104.0 0.6 fusion.7
  104.6 1.4 fusion.16
  106.1 0.1 fusion.28
  106.1 2.3 %convolution_convert_fusion.own_ref = bf16[2048,384]{1,0:T(8,128)(2,1)} fusion(bf16[288,384]{1,0:T(8,128)(2,1)S(1)} %bitcast.55, bf16[192,2048]{1,0:T(8,128)(2,1)S(1)} %fusion.28, bf16[96,2048]{1,0:T(8,128)(2,1)S(1)} %bitcast.71), kind=kOutput, calls=%fused_computation.11 | convolution fusion | flops 456130560 | bytes 2973696 | tf_op jit(solution)/shard_map/dot_general | solution.py:465
  108.5 0.8 convolution_convert_fusion.2.low_ref
  109.2 1.9 %convolution_convert_fusion.1.high_ref = bf16[2048,384]{1,0:T(8,128)(2,1)} fusion(bf16[192,384]{1,0:T(8,128)(2,1)S(1)} %bitcast.68, bf16[96,6144]{1,0:T(8,128)(2,1)S(1)} %fusion.7, bf16[96,6144]{1,0:T(8,128)(2,1)S(1)} %get-tuple-element.25), kind=kOutput, calls=%fused_computation.12 | convolution fusion | flops 304349184 | bytes 4079616 | tf_op jit(solution)/shard_map/dot_general | solution.py:465
  111.1 0.0 copy-start.4
  111.1 0.0 copy-start.9
  111.1 48.1 %shard_map.112 = (bf16[384,512]{1,0:T(8,128)(2,1)S(1)}, f32[512,384]{1,0:T(8,128)S(1)}, f32[288,384]{1,0:T(8,128)S(1)}, f32[384,384]{1,0:T(8,128)S(1)}, f32[8,384]{1,0:T(8,128)S(1)}) custom-call(bf16[96,2048]{1,0:T(8,128)(2,1)S(1)} %get-tuple-element.17.att_ref, bf16[512,384]{1,0:T(8,128)(2,1)S(1)} %copy-done.1, ...), custom_call_target="tpu_custom_call" | custom-call | tf_op jit(solution)/shard_map/pallas_call | solution.py:429
  159.2 0.0 copy-done.4
  159.2 1.2 fusion.12
  160.4 0.6 slice_reduce_fusion
  161.0 0.0 copy-done.9
  161.0 0.2 fusion.25
  161.2 1.1 fusion.24
  162.3 0.8 copy.20
  163.1 0.8 copy.21
  (9 shorter events, 0.1 us)
Async XLA Ops:
  0.6 2.8 %copy-start = (bf16[3,384,384]{2,1,0:T(8,128)(2,1)S(1)}, bf16[3,384,384]{2,1,0:T(8,128)(2,1)}, u32[]{:S(2)}) copy-start(bf16[3,384,384]{2,1,0:T(8,128)(2,1)} %param.9) | copy-start | bytes 2654212
  0.6 4.3 %copy-start.1 = (bf16[512,384]{1,0:T(8,128)(2,1)S(1)}, bf16[512,384]{1,0:T(8,128)(2,1)}, u32[]{:S(2)}) copy-start(bf16[512,384]{1,0:T(8,128)(2,1)} %cot_ref.1) | copy-start | bytes 1179652
  0.7 4.3 %copy-start.8 = (bf16[384,384]{1,0:T(8,128)(2,1)S(1)}, bf16[384,384]{1,0:T(8,128)(2,1)}, u32[]{:S(2)}) copy-start(bf16[384,384]{1,0:T(8,128)(2,1)} %param.10) | copy-start | bytes 884740
  45.4 2.8 %copy-start.3 = (f32[192,6144]{1,0:T(8,128)}, f32[192,6144]{1,0:T(8,128)S(1)}, u32[]{:S(2)}) copy-start(f32[192,6144]{1,0:T(8,128)S(1)} %fusion.37) | copy-start | bytes 14155780
  45.7 1.6 copy-start.5
  48.5 1.6 copy-start.2
  97.1 1.7 %copy-start.7 = (bf16[192,6144]{1,0:T(8,128)(2,1)S(1)}, bf16[192,6144]{1,0:T(8,128)(2,1)}, u32[]{:S(2)}) copy-start(bf16[192,6144]{1,0:T(8,128)(2,1)} %get-tuple-element.18) | copy-start | bytes 7077892
  97.4 2.2 %copy-start.6 = (f32[96,6144]{1,0:T(8,128)S(1)}, f32[96,6144]{1,0:T(8,128)}, u32[]{:S(2)}) copy-start(f32[96,6144]{1,0:T(8,128)} %copy-done.5) | copy-start | bytes 7077892
  98.8 5.2 %slice-start = ((s8[4718592]{0:T(1024)(128)(4,1)}), s8[4194304]{0:T(1024)(128)(4,1)S(1)}, s32[]{:S(2)}) async-start(s8[4718592]{0:T(1024)(128)(4,1)} %bitcast.60), calls=%async_computation | async-start | bytes 8388608
  99.5 4.4 %slice-start.1 = ((s8[4718592]{0:T(1024)(128)(4,1)}), s8[524288]{0:T(1024)(128)(4,1)S(1)}, s32[]{:S(2)}) async-start(s8[4718592]{0:T(1024)(128)(4,1)} %bitcast.60), calls=%async_computation.1 | async-start | bytes 1048576
  111.1 48.1 %copy-start.4 = (bf16[512,384]{1,0:T(8,128)(2,1)S(1)}, bf16[512,384]{1,0:T(8,128)(2,1)}, u32[]{:S(2)}) copy-start(bf16[512,384]{1,0:T(8,128)(2,1)} %param.7) | copy-start | bytes 1179652
  111.1 49.9 %copy-start.9 = (f32[384]{0:T(512)S(1)}, f32[384]{0:T(512)}, u32[]{:S(2)}) copy-start(f32[384]{0:T(512)} %param.8) | copy-start | bytes 4612

commit v4 on v3

--- a/solution.py
+++ b/solution.py
@@ -32,7 +32,7 @@
     wide = n_heads * BLK
     ext = kv_ref.shape[1] // BLK
 
-    @pl.loop(0, ext)
+    @pl.loop(0, ext, unroll=8)
     def _(i):
         both = kv_ref[:, pl.ds(pl.multiple_of(i * BLK, BLK), BLK)]
         kv_t[i] = both
@@ -54,8 +54,7 @@
     def of_head(value, h):
         return value[h * hd : (h + 1) * hd, h * BLK : (h + 1) * BLK]
 
-    @pl.loop(0, q_ref.shape[1] // BLK)
-    def _(b):
+    def scores(b, e_s):
         at = pl.ds(pl.multiple_of(b * BLK, BLK), BLK)
         q_t = q_ref[:, at]
         do_t = do_ref[:, at]
@@ -68,6 +67,10 @@
             raised = raised * jnp.where(j < count, 1.0, 0.0)
             total = total + jnp.sum(raised, axis=0, keepdims=True)
             e_s[j * BLK : (j + 1) * BLK, :] = raised.astype(BF16)
+        return at, q_t, do_t, slots, q_diag, total
+
+    def middle(state, e_s):
+        at, q_t, do_t, slots, q_diag, total = state
         values_t = jnp.concatenate([kv_t[s][cols:] for s in slots], axis=1)
         keys_t = jnp.concatenate([kv_t[s][:cols] for s in slots], axis=1)
         out = dot(values_t, e_s[...])
@@ -85,6 +88,10 @@
         do_diag = diagonal(scaled)
         q_rows = q_diag.T
         do_rows = do_diag.T
+        return at, slots, keys_t, do_diag, q_rows, do_rows, inner
+
+    def backward(state, e_s, ds_s):
+        at, slots, keys_t, do_diag, q_rows, do_rows, inner = state
         for j in range(n_slots):
             rows = slice(j * BLK, (j + 1) * BLK)
             e = e_s[rows, :]
@@ -97,7 +104,16 @@
         dq = jnp.concatenate([of_head(dq, h) for h in range(n_heads)], axis=0)
         dq_ref[:, at] = (dq * SCORE_SCALE).astype(dq_ref.dtype)
 
-    @pl.loop(0, ext)
+    @pl.loop(0, q_ref.shape[1] // BLK, step=2)
+    def _(b):
+        one = scores(b, e_s.at[0])
+        two = scores(b + 1, e_s.at[1])
+        one = middle(one, e_s.at[0])
+        two = middle(two, e_s.at[1])
+        backward(one, e_s.at[0], ds_s.at[0])
+        backward(two, e_s.at[1], ds_s.at[1])
+
+    @pl.loop(0, ext, unroll=8)
     def _(i):
         at = pl.ds(pl.multiple_of(i * BLK, BLK), BLK)
         g_ref[:cols, at] = (dk_acc[i] * math.log(2.0)).T.astype(g_ref.dtype)
@@ -127,8 +143,8 @@
             pltpu.VMEM((ext, BLK, cols), BF16),
             pltpu.VMEM((ext, BLK, cols), F32),
             pltpu.VMEM((ext, BLK, cols), F32),
-            pltpu.VMEM((n_slots * BLK, n_heads * BLK), BF16),
-            pltpu.VMEM((n_slots * BLK, n_heads * BLK), BF16),
+            pltpu.VMEM((2, n_slots * BLK, n_heads * BLK), BF16),
+            pltpu.VMEM((2, n_slots * BLK, n_heads * BLK), BF16),
         ],
         compiler_params=pltpu.CompilerParams(vmem_limit_bytes=52 * 1024 * 1024),
     )(lookup, counts, q_t, do_t, kv_ext)

time: 164 us -> 155 us (0.945)
  Pallas kernels: 132 us -> 123 us
    pallas_call x1, Pallas kernels: 47 us -> 37.8 us  [attention(): pl.pallas_call(functools.partial(attention_kernel, n_heads, hd, n_slots),...]
where the time goes in v4:
time: 155 us
  Pallas kernels  123 us (79%)
  other arithmetic  11.9 us (8%)
  matrix products  10.8 us (7%)
  local copies, waits for them, and re-layouts  8.1 us (5%)
    pallas_call x1, Pallas kernels, grad_sums(): pl.pallas_call(functools.partial(sums_kernel, n_slab, n_head), out_shape=...  48.1 us
    pallas_call x1, Pallas kernels, attention(): pl.pallas_call(functools.partial(attention_kernel, n_heads, hd, n_slots),...  37.8 us
    pallas_call x1, Pallas kernels, gather_slabs(): pl.pallas_call(functools.partial(gather_kernel, n_slab, n_head), out_shap...  37.2 us
    dot_general x4, matrix products, over_rows(): lax.dot_general(a, b, (((0,), (0,)), ((), ())), preferred_element_type=F32)  6.2 us
    unnamed x28, local copies, waits for them, and re-layouts  6.07 us
    mul x2, other arithmetic, unit_back(): result = (along - jnp.where(active, unit * inner, 0.0)) / divisor  4.85 us

profile of v4, /device:TPU:0, one launch (start us, length us, event | category | flops | bytes accessed | tf_op | source)
XLA Modules:
  0.0 154.9 jit_solution(841403237824294515)
XLA Ops:
  0.6 0.0 copy-start
  0.6 0.0 copy-start.1
  0.7 0.0 copy-start.8
  0.7 0.8 broadcast_in_dim.41.gain_ref
  1.5 1.1 fusion.19
  2.6 0.8 copy.15
  3.4 0.0 copy-done
  3.4 0.2 constant_dynamic-slice_fusion
  3.6 0.2 copy.17
  3.8 1.2 fusion.21.normed_ref
  5.0 0.0 copy-done.1
  5.0 0.0 copy-done.8
  5.0 0.4 convolution_convert_fusion.3.d_att_ref
  5.4 37.2 %shard_map.110 = (bf16[3,4,512,384]{3,2,1,0:T(8,128)(2,1)S(1)}, bf16[96,2048]{1,0:T(8,128)(2,1)S(1)}) custom-call(bf16[512,384]{1,0:T(8,128)(2,1)S(1)} %fusion.21.normed_ref, bf16[384,512]{1,0:T(8,128)(2,1)S(1)} %convolution_convert_fusion.3.d_att_ref), custom_call_target="tpu_custom_call" | custom-call | tf_op jit(solution)/shard_map/pallas_call | solution.py:248
  42.6 0.2 slice.44
  42.8 0.6 multiply_reduce_fusion.2
  43.5 0.1 multiply_convert_fusion
  43.6 1.8 %fusion.37 = f32[192,6144]{1,0:T(8,128)S(1)} fusion(bf16[192,384]{1,0:T(8,128)(2,1)S(1)} %bitcast.66, bf16[6144,384]{1,0:T(8,128)(2,1)S(1)} %bitcast.51), kind=kOutput, calls=%fused_computation.78 | convolution fusion | flops 905969664 | bytes 9584640 | tf_op jit(solution)/shard_map/dot_general | solution.py:485
  45.4 0.0 copy-start.3
  45.4 0.1 slice.95
  45.6 0.2 slice.58
  45.7 0.0 copy-start.5
  45.7 1.6 %copy-done.5 = f32[96,6144]{1,0:T(8,128)} copy-done((f32[96,6144]{1,0:T(8,128)}, f32[96,6144]{1,0:T(8,128)S(1)}, u32[]{:S(2)}) %copy-start.5) | copy-done | bytes 2359320
  47.4 0.3 multiply_reduce_fusion.1
  47.7 0.1 sqrt_compare_fusion
  47.8 0.1 sqrt_maximum_fusion
  47.8 0.4 copy-done.3
  48.3 0.2 fusion.18
  48.5 0.0 copy-start.2
  48.5 1.6 %pad_maximum_fusion.2.kv_ref = bf16[192,6144]{1,0:T(8,128)(2,1)} fusion(bf16[96,6144]{1,0:T(8,128)(2,1)S(1)} %slice.95, bf16[96,6144]{1,0:T(8,128)(2,1)S(1)} %fusion.18), kind=kLoop, calls=%fused_computation.21 | loop fusion | flops 4718592 | bytes 4718592 | tf_op jit(solution)/shard_map/concatenate | solution.py:526
  50.1 0.0 copy-done.2
  50.1 37.8 %shard_map.111 = (bf16[96,2048]{1,0:T(8,128)(2,1)S(1)}, bf16[96,2048]{1,0:T(8,128)(2,1)S(1)}, bf16[192,6144]{1,0:T(8,128)(2,1)}) custom-call(s32[16,8]{1,0:T(8,128)S(1)} %add_select_fusion.lookup_ref, s32[16]{0:T(128)S(1)} %copy-done.2, bf16[96,2048]{1,0:T(8,128)(2,1)S(1)} %bitcast.57, bf16[96,2048]{1,0:T(8,128)(2,1)S(1)} %get-tuple-element.16.do_ref, ...), custom_call_target="tpu_custom_call" | custom-call | tf_op jit(solution)/shard_map/pallas_call | solution.py:131
  87.9 0.0 copy-start.7
  87.9 0.3 fusion.11
  88.2 0.0 copy-start.6
  88.2 0.4 convolution_convert_fusion.4
  88.6 1.0 copy-done.7
  89.6 0.0 slice-start
  89.6 0.3 fusion.36
  89.9 0.5 copy-done.6
  90.4 0.0 slice-start.1
  90.4 4.6 %fusion.1 = f32[3,32,6144]{2,1,0:T(8,128)S(1)} fusion(f32[3,32,6144]{2,1,0:T(8,128)S(1)} %bitcast.69, f32[3,32,6144]{2,1,0:T(8,128)S(1)} %bitcast.65, f32[3,6144]{1,0:T(4,128)S(1)} %sqrt_maximum_fusion), kind=kOutput, calls=%fused_computation.1 | output fusion | flops 1198111 | bytes 7151616 | tf_op jit(solution)/shard_map/mul | solution.py:519
  94.9 0.0 slice-done
  95.0 0.0 slice-done.1
  95.0 0.6 fusion.7
  95.6 1.4 fusion.16
  97.1 0.1 fusion.28
  97.1 2.3 %convolution_convert_fusion.own_ref = bf16[2048,384]{1,0:T(8,128)(2,1)} fusion(bf16[288,384]{1,0:T(8,128)(2,1)S(1)} %bitcast.55, bf16[192,2048]{1,0:T(8,128)(2,1)S(1)} %fusion.28, bf16[96,2048]{1,0:T(8,128)(2,1)S(1)} %bitcast.71), kind=kOutput, calls=%fused_computation.11 | convolution fusion | flops 456130560 | bytes 2973696 | tf_op jit(solution)/shard_map/dot_general | solution.py:481
  99.5 0.8 convolution_convert_fusion.2.low_ref
  100.2 1.9 %convolution_convert_fusion.1.high_ref = bf16[2048,384]{1,0:T(8,128)(2,1)} fusion(bf16[192,384]{1,0:T(8,128)(2,1)S(1)} %bitcast.68, bf16[96,6144]{1,0:T(8,128)(2,1)S(1)} %fusion.7, bf16[96,6144]{1,0:T(8,128)(2,1)S(1)} %get-tuple-element.25), kind=kOutput, calls=%fused_computation.12 | convolution fusion | flops 304349184 | bytes 4079616 | tf_op jit(solution)/shard_map/dot_general | solution.py:481
  102.1 0.0 copy-start.4
  102.1 0.0 copy-start.9
  102.1 48.1 %shard_map.112 = (bf16[384,512]{1,0:T(8,128)(2,1)S(1)}, f32[512,384]{1,0:T(8,128)S(1)}, f32[288,384]{1,0:T(8,128)S(1)}, f32[384,384]{1,0:T(8,128)S(1)}, f32[8,384]{1,0:T(8,128)S(1)}) custom-call(bf16[96,2048]{1,0:T(8,128)(2,1)S(1)} %get-tuple-element.17.att_ref, bf16[512,384]{1,0:T(8,128)(2,1)S(1)} %copy-done.1, ...), custom_call_target="tpu_custom_call" | custom-call | tf_op jit(solution)/shard_map/pallas_call | solution.py:445
  150.2 0.0 copy-done.4
  150.2 1.2 fusion.12
  151.4 0.6 slice_reduce_fusion
  152.0 0.0 copy-done.9
  152.0 0.2 fusion.25
  152.2 1.1 fusion.24
  153.3 0.8 copy.20
  154.1 0.8 copy.21
  (9 shorter events, 0.1 us)
Async XLA Ops:
  0.6 2.8 %copy-start = (bf16[3,384,384]{2,1,0:T(8,128)(2,1)S(1)}, bf16[3,384,384]{2,1,0:T(8,128)(2,1)}, u32[]{:S(2)}) copy-start(bf16[3,384,384]{2,1,0:T(8,128)(2,1)} %param.9) | copy-start | bytes 2654212
  0.6 4.3 %copy-start.1 = (bf16[512,384]{1,0:T(8,128)(2,1)S(1)}, bf16[512,384]{1,0:T(8,128)(2,1)}, u32[]{:S(2)}) copy-start(bf16[512,384]{1,0:T(8,128)(2,1)} %cot_ref.1) | copy-start | bytes 1179652
  0.7 4.3 %copy-start.8 = (bf16[384,384]{1,0:T(8,128)(2,1)S(1)}, bf16[384,384]{1,0:T(8,128)(2,1)}, u32[]{:S(2)}) copy-start(bf16[384,384]{1,0:T(8,128)(2,1)} %param.10) | copy-start | bytes 884740
  45.4 2.8 %copy-start.3 = (f32[192,6144]{1,0:T(8,128)}, f32[192,6144]{1,0:T(8,128)S(1)}, u32[]{:S(2)}) copy-start(f32[192,6144]{1,0:T(8,128)S(1)} %fusion.37) | copy-start | bytes 14155780
  45.7 1.6 %copy-start.5 = (f32[96,6144]{1,0:T(8,128)}, f32[96,6144]{1,0:T(8,128)S(1)}, u32[]{:S(2)}) copy-start(f32[96,6144]{1,0:T(8,128)S(1)} %slice.58) | copy-start | bytes 7077892
  48.5 1.6 %copy-start.2 = (s32[16]{0:T(128)S(1)}, s32[16]{0:T(128)}, u32[]{:S(2)}) copy-start(s32[16]{0:T(128)} %counts_ref.1) | copy-start | bytes 196
  87.9 1.7 %copy-start.7 = (bf16[192,6144]{1,0:T(8,128)(2,1)S(1)}, bf16[192,6144]{1,0:T(8,128)(2,1)}, u32[]{:S(2)}) copy-start(bf16[192,6144]{1,0:T(8,128)(2,1)} %get-tuple-element.18) | copy-start | bytes 7077892
  88.2 2.2 %copy-start.6 = (f32[96,6144]{1,0:T(8,128)S(1)}, f32[96,6144]{1,0:T(8,128)}, u32[]{:S(2)}) copy-start(f32[96,6144]{1,0:T(8,128)} %copy-done.5) | copy-start | bytes 7077892
  89.6 5.4 %slice-start = ((s8[4718592]{0:T(1024)(128)(4,1)}), s8[4194304]{0:T(1024)(128)(4,1)S(1)}, s32[]{:S(2)}) async-start(s8[4718592]{0:T(1024)(128)(4,1)} %bitcast.60), calls=%async_computation | async-start | bytes 8388608
  90.4 4.6 %slice-start.1 = ((s8[4718592]{0:T(1024)(128)(4,1)}), s8[524288]{0:T(1024)(128)(4,1)S(1)}, s32[]{:S(2)}) async-start(s8[4718592]{0:T(1024)(128)(4,1)} %bitcast.60), calls=%async_computation.1 | async-start | bytes 1048576
  102.1 48.1 %copy-start.4 = (bf16[512,384]{1,0:T(8,128)(2,1)S(1)}, bf16[512,384]{1,0:T(8,128)(2,1)}, u32[]{:S(2)}) copy-start(bf16[512,384]{1,0:T(8,128)(2,1)} %param.7) | copy-start | bytes 1179652
  102.1 49.9 %copy-start.9 = (f32[384]{0:T(512)S(1)}, f32[384]{0:T(512)}, u32[]{:S(2)}) copy-start(f32[384]{0:T(512)} %param.8) | copy-start | bytes 4612
